TPU v7x, 128 devices: a whole 4x4x4 slice. The times are simulated.
128 devices in a mesh: ep: 128 (over z, y, x, core).
Axes of the slice: x: 4, y: 4, z: 4, core: 2. Of those that a mesh axis runs over, the one named last changes fastest.
Arguments:
- tokens: bfloat16 [16384, 1024], P('ep'), may hold values from -6 to 6
- cotangent: bfloat16 [16384, 1024], P('ep'), may hold values from -6 to 6
- routes: int32 [16384, 8], P('ep'), may hold values from 0 to 127, all different within a row; in each aligned block of 128 rows (0 to 127, 128 to 255, ...) at most 12 rows name the same one
- gate_weights: float32 [16384, 8], P('ep'), may hold values from 0.05 to 0.5
- old_experts: int32 [128], replicated, may hold values from 0 to 63
- source: int32 [128], replicated, may hold values from 0 to 127
- gate_up_weight: bfloat16 [128, 1024, 1024], P('ep'), may hold values from -0.1875 to 0.1875
- down_weight: bfloat16 [128, 512, 1024], P('ep'), may hold values from -0.25 to 0.25
- first_gate_up: bfloat16 [128, 1024, 1024], P('ep'), may hold values from -18 to 18
- first_down: bfloat16 [128, 512, 1024], P('ep'), may hold values from -18 to 18
- second_gate_up: bfloat16 [128, 1024, 1024], P('ep'), may hold values from 1 to 100
- second_down: bfloat16 [128, 512, 1024], P('ep'), may hold values from 1 to 100
Outputs:
- layer_out: bfloat16 [16384, 1024], P('ep')
- new_gate_up: bfloat16 [128, 1024, 1024], P('ep')
- new_down: bfloat16 [128, 512, 1024], P('ep')
- new_first_gate_up: bfloat16 [128, 1024, 1024], P('ep')
- new_first_down: bfloat16 [128, 512, 1024], P('ep')
- new_second_gate_up: bfloat16 [128, 1024, 1024], P('ep')
- new_second_down: bfloat16 [128, 512, 1024], P('ep')
Inputs may be any that keep to these rules, and one draw needn't show every extreme that they name: `routes`: the 8 slots of a token differ; among the rows of one device no slot is named more than 12 times, a bound that some block reaches.
All inputs are finite; a program needn't handle non-finite values.
Results may differ from a plain program's by a relative error of at most 0.0058.
Values may be sent and summed in bfloat16 or wider, within the bound.
A program may use at most 128 MiB of HBM per device.

v0:
```python
import jax
import jax.numpy as jnp
from jax import lax
from jax.sharding import PartitionSpec as P


def for_sending(value):

    def short(part):
        return part.astype(jnp.bfloat16) if part.dtype == jnp.float32 else part

    return jax.tree.map(short, value)


def positions(flat_routes, n_slots):
    onehot = (flat_routes[:, None] == jnp.arange(n_slots, dtype=jnp.int32)[None, :]).astype(
        jnp.int32
    )
    before = jnp.cumsum(onehot, axis=0) - onehot
    return jnp.sum(before * onehot, axis=1)


def forward_backward(rows_x, rows_dy, gate_up, down_part):
    hidden_width = down_part.shape[0]
    pre_act = jnp.dot(rows_x, gate_up, preferred_element_type=jnp.float32)
    gate_pre = pre_act[:, :hidden_width]
    up_part = pre_act[:, hidden_width:]
    sigmoid_gate = jax.nn.sigmoid(gate_pre)
    activated = gate_pre * sigmoid_gate
    hidden = (activated * up_part).astype(jnp.bfloat16)
    output = jnp.dot(hidden, down_part, preferred_element_type=jnp.float32).astype(jnp.bfloat16)
    d_hidden = jnp.dot(rows_dy, down_part.T, preferred_element_type=jnp.float32)
    d_gate = d_hidden * up_part * sigmoid_gate * (1.0 + gate_pre * (1.0 - sigmoid_gate))
    d_up = d_hidden * activated
    d_pre = jnp.concatenate([d_gate, d_up], axis=1).astype(jnp.bfloat16)
    grad_gate_up = jnp.dot(rows_x.T, d_pre, preferred_element_type=jnp.float32)
    grad_down = jnp.dot(hidden.T, rows_dy, preferred_element_type=jnp.float32)
    return (output, grad_gate_up, grad_down)


def adam_update(weight, first_moment, second_moment, gradient):
    first_new = 0.9 * first_moment.astype(jnp.float32) + 0.1 * gradient
    second_new = 0.95 * second_moment.astype(jnp.float32) + 0.05 * gradient * gradient
    weight_new = weight.astype(jnp.float32) - 0.01 * first_new / (jnp.sqrt(second_new) + 1e-08)
    return (
        weight_new.astype(jnp.bfloat16),
        first_new.astype(jnp.bfloat16),
        second_new.astype(jnp.bfloat16),
    )


def shards(
    tokens,
    cotangent,
    routes,
    gate_weights,
    old_experts,
    source,
    gate_up_weight,
    down_weight,
    first_gate_up,
    first_down,
    second_gate_up,
    second_down,
):
    n_slots = lax.axis_size("ep")
    tok_rows, model_width = tokens.shape
    top_count = routes.shape[1]
    capacity = 3 * tok_rows * top_count // (2 * n_slots)
    gate_up_shape = gate_up_weight.shape
    down_shape = down_weight.shape

    def split_up(gate_up):
        return gate_up.reshape(n_slots, gate_up_shape[1] // n_slots, gate_up_shape[2])

    def split_down(down_part):
        return down_part.reshape(n_slots, down_shape[1] // n_slots, down_shape[2])

    pieces = (
        lax.all_to_all(split_up(gate_up_weight), "ep", split_axis=0, concat_axis=0, tiled=True),
        lax.all_to_all(split_down(down_weight), "ep", split_axis=0, concat_axis=0, tiled=True),
        lax.all_to_all(split_up(first_gate_up), "ep", split_axis=0, concat_axis=0, tiled=True),
        lax.all_to_all(split_down(first_down), "ep", split_axis=0, concat_axis=0, tiled=True),
        lax.all_to_all(split_up(second_gate_up), "ep", split_axis=0, concat_axis=0, tiled=True),
        lax.all_to_all(split_down(second_down), "ep", split_axis=0, concat_axis=0, tiled=True),
    )
    chosen = tuple((jnp.take(shard_piece, source, axis=0) for shard_piece in pieces))
    flat_routes = routes.reshape(-1)
    target = flat_routes * capacity + positions(flat_routes, n_slots)
    scaled = (
        (gate_weights[:, :, None] * cotangent[:, None, :].astype(jnp.float32))
        .astype(jnp.bfloat16)
        .reshape(-1, model_width)
    )
    empty_rows = jnp.zeros((n_slots * capacity, model_width), jnp.bfloat16)
    send_x = (
        empty_rows.at[target]
        .set(jnp.repeat(tokens, top_count, axis=0))
        .reshape(n_slots, capacity, model_width)
    )
    send_dy = empty_rows.at[target].set(scaled).reshape(n_slots, capacity, model_width)
    rows_x, rows_dy = (
        lax.all_to_all(send_x, "ep", split_axis=0, concat_axis=0, tiled=True),
        lax.all_to_all(send_dy, "ep", split_axis=0, concat_axis=0, tiled=True),
    )
    rows_x = rows_x.reshape(-1, model_width)
    rows_dy = rows_dy.reshape(-1, model_width)
    home_state = jax.tree.map(
        lambda part, own: part.astype(own.dtype),
        lax.all_to_all(for_sending(chosen), "ep", split_axis=0, concat_axis=0, tiled=True),
        chosen,
    )
    gate_up_now = home_state[0].reshape(gate_up_shape[1:])
    down_now = home_state[1].reshape(down_shape[1:])
    output, grad_gate_up, grad_down = forward_backward(rows_x, rows_dy, gate_up_now, down_now)
    returned = lax.all_to_all(
        output.reshape(n_slots, capacity, model_width),
        "ep",
        split_axis=0,
        concat_axis=0,
        tiled=True,
    )
    picked = (
        returned.reshape(-1, model_width)[target]
        .astype(jnp.float32)
        .reshape(tok_rows, top_count, model_width)
    )
    layer_out = jnp.sum(gate_weights[:, :, None] * picked, axis=1).astype(jnp.bfloat16)
    grad_parts = (
        lax.all_to_all(split_up(grad_gate_up), "ep", split_axis=0, concat_axis=0, tiled=True),
        lax.all_to_all(split_down(grad_down), "ep", split_axis=0, concat_axis=0, tiled=True),
    )
    new_expert = old_experts[source]
    same_expert = (new_expert[:, None] == new_expert[None, :]).astype(jnp.float32)
    summed_up = jnp.einsum(
        "st,trc->src", same_expert, grad_parts[0], precision=lax.Precision.HIGHEST
    )
    summed_down = jnp.einsum(
        "st,trc->src", same_expert, grad_parts[1], precision=lax.Precision.HIGHEST
    )
    total_up, total_down = (
        lax.all_to_all(summed_up, "ep", split_axis=0, concat_axis=0, tiled=True),
        lax.all_to_all(summed_down, "ep", split_axis=0, concat_axis=0, tiled=True),
    )
    up_final = adam_update(home_state[0], home_state[2], home_state[4], total_up)
    down_final = adam_update(home_state[1], home_state[3], home_state[5], total_down)
    finals = (up_final[0], down_final[0], up_final[1], down_final[1], up_final[2], down_final[2])
    new_gate_up = finals[0].reshape(gate_up_shape)
    new_down = finals[1].reshape(down_shape)
    new_first_gate_up = finals[2].reshape(gate_up_shape)
    new_first_down = finals[3].reshape(down_shape)
    new_second_gate_up = finals[4].reshape(gate_up_shape)
    new_second_down = finals[5].reshape(down_shape)
    return (
        layer_out,
        new_gate_up,
        new_down,
        new_first_gate_up,
        new_first_down,
        new_second_gate_up,
        new_second_down,
    )


def solution(mesh):
    in_specs = (
        P("ep", None),
        P("ep", None),
        P("ep", None),
        P("ep", None),
        P(),
        P(),
        P("ep", None, None),
        P("ep", None, None),
        P("ep", None, None),
        P("ep", None, None),
        P("ep", None, None),
        P("ep", None, None),
    )
    out_specs = (
        P("ep", None),
        P("ep", None, None),
        P("ep", None, None),
        P("ep", None, None),
        P("ep", None, None),
        P("ep", None, None),
        P("ep", None, None),
    )
    return jax.shard_map(shards, mesh=mesh, in_specs=in_specs, out_specs=out_specs, check_vma=False)
```

profile of v0, /device:TPU:1, one launch (start us, length us, event | category | flops | bytes accessed | tf_op | source)
XLA Modules:
  0.0 739.3 jit_solution(16311804818940907361)
XLA Ops:
  3.0 11.5 %all-to-all-start.3 = ((bf16[128,4,1024]{2,1,0:T(4,128)(2,1)}), bf16[128,4,1024]{2,1,0:T(4,128)(2,1)S(1)}, u32[]{:S(2)}, u32[]{:S(2)}) async-start(bf16[128,4,1024]{2,1,0:T(4,128)(2,1)} %reshape.155), calls=%async_computation.3 | async-start | bytes 2097152 | tf_op jit(solution)/shard_map/all_to_all | solution.py:81
  15.7 18.1 %all-to-all-done.3 = bf16[128,4,1024]{2,1,0:T(4,128)(2,1)S(1)} async-done(((bf16[128,4,1024]{2,1,0:T(4,128)(2,1)}), bf16[128,4,1024]{2,1,0:T(4,128)(2,1)S(1)}, u32[]{:S(2)}, u32[]{:S(2)}) %all-to-all-start.3) | async-done | bytes 1048608 | tf_op jit(solution)/shard_map/all_to_all | solution.py:81
  39.7 18.0 %all-to-all-done.13 = bf16[128,4,1024]{2,1,0:T(4,128)(2,1)S(1)} async-done(((bf16[128,4,1024]{2,1,0:T(4,128)(2,1)}), bf16[128,4,1024]{2,1,0:T(4,128)(2,1)S(1)}, u32[]{:S(2)}, u32[]{:S(2)}) %all-to-all-start.13) | async-done | bytes 1048608 | tf_op jit(solution)/shard_map/all_to_all | solution.py:83
  57.6 23.9 %all_to_all.95 = bf16[128,4,1024]{2,1,0:T(4,128)(2,1)} all-to-all(bf16[128,4,1024]{2,1,0:T(4,128)(2,1)S(1)} %reshape.165), channel_id=1, replica_groups=mesh['ep'=128] {'ep'}, dimensions={0} | all-to-all | bytes 2097152 | tf_op jit(solution)/shard_map/all_to_all | solution.py:85
  81.6 35.1 %all_to_all.96 = bf16[128,8,1024]{2,1,0:T(8,128)(2,1)} all-to-all(bf16[128,8,1024]{2,1,0:T(8,128)(2,1)S(1)} %bitcast.57), channel_id=1, replica_groups=mesh['ep'=128] {'ep'}, dimensions={0} | all-to-all | bytes 4194304 | tf_op jit(solution)/shard_map/all_to_all | solution.py:80
  116.7 35.0 %all_to_all.97 = bf16[128,8,1024]{2,1,0:T(8,128)(2,1)} all-to-all(bf16[128,8,1024]{2,1,0:T(8,128)(2,1)S(1)} %bitcast.58), channel_id=1, replica_groups=mesh['ep'=128] {'ep'}, dimensions={0} | all-to-all | bytes 4194304 | tf_op jit(solution)/shard_map/all_to_all | solution.py:82
  151.8 4.5 all-to-all-start.11
  170.1 16.8 %all-to-all-done.11 = bf16[128,8,1024]{2,1,0:T(8,128)(2,1)S(1)} async-done(((bf16[128,8,1024]{2,1,0:T(8,128)(2,1)}), bf16[128,8,1024]{2,1,0:T(8,128)(2,1)S(1)}, u32[]{:S(2)}, u32[]{:S(2)}) %all-to-all-start.11) | async-done | bytes 2097184 | tf_op jit(solution)/shard_map/all_to_all | solution.py:84
  186.9 24.9 %all_to_all.98 = bf16[128,4,1024]{2,1,0:T(4,128)(2,1)} all-to-all(bf16[128,4,1024]{2,1,0:T(4,128)(2,1)} %get-tuple-element.18), channel_id=1, replica_groups=mesh['ep'=128] {'ep'}, dimensions={0} | all-to-all | bytes 2097152 | tf_op jit(solution)/shard_map/all_to_all | solution.py:110
  217.0 18.6 %all-to-all-done.14 = bf16[128,4,1024]{2,1,0:T(4,128)(2,1)S(1)} async-done(((bf16[128,4,1024]{2,1,0:T(4,128)(2,1)}), bf16[128,4,1024]{2,1,0:T(4,128)(2,1)S(1)}, u32[]{:S(2)}, u32[]{:S(2)}) %all-to-all-start.14) | async-done | bytes 1048608 | tf_op jit(solution)/shard_map/all_to_all | solution.py:110
  235.6 5.9 all-to-all-start.4
  243.2 7.0 scatter_custom_fusion.1
  253.0 7.5 %all-to-all-done.4 = bf16[128,4,1024]{2,1,0:T(4,128)(2,1)} async-done(((bf16[128,4,1024]{2,1,0:T(4,128)(2,1)}), bf16[128,4,1024]{2,1,0:T(4,128)(2,1)}, u32[]{:S(2)}, u32[]{:S(2)}) %all-to-all-start.4) | async-done | bytes 1048608 | tf_op jit(solution)/shard_map/all_to_all | solution.py:110
  260.5 5.4 all-to-all-start.8
  265.9 6.3 scatter_custom_fusion
  275.0 43.7 %all-to-all-done.8 = bf16[128,12,1024]{2,1,0:T(8,128)(2,1)} async-done(((bf16[128,12,1024]{2,1,0:T(8,128)(2,1)}), bf16[128,12,1024]{2,1,0:T(8,128)(2,1)}, u32[]{:S(2)}, u32[]{:S(2)}) %all-to-all-start.8) | async-done | bytes 3145760 | tf_op jit(solution)/shard_map/all_to_all | solution.py:104
  318.7 5.5 all-to-all-start
  331.9 4.6 broadcast_select_fusion.1
  336.5 40.5 %all-to-all-done = bf16[128,12,1024]{2,1,0:T(8,128)(2,1)} async-done(((bf16[128,12,1024]{2,1,0:T(8,128)(2,1)}), bf16[128,12,1024]{2,1,0:T(8,128)(2,1)}, u32[]{:S(2)}, u32[]{:S(2)}) %all-to-all-start) | async-done | bytes 3145760 | tf_op jit(solution)/shard_map/all_to_all | solution.py:103
  377.0 35.4 %all_to_all.99 = bf16[128,8,1024]{2,1,0:T(8,128)(2,1)} all-to-all(bf16[128,8,1024]{2,1,0:T(8,128)(2,1)S(1)} %get-tuple-element.21), channel_id=1, replica_groups=mesh['ep'=128] {'ep'}, dimensions={0} | all-to-all | bytes 4194304 | tf_op jit(solution)/shard_map/all_to_all | solution.py:110
  412.4 5.4 all-to-all-start.2
  420.0 6.1 reshape.273
  426.1 6.1 reshape.161
  432.3 4.7 reshape.152
  437.0 11.2 %all-to-all-done.2 = bf16[128,8,1024]{2,1,0:T(8,128)(2,1)} async-done(((bf16[128,8,1024]{2,1,0:T(8,128)(2,1)}), bf16[128,8,1024]{2,1,0:T(8,128)(2,1)}, u32[]{:S(2)}, u32[]{:S(2)}) %all-to-all-start.2) | async-done | bytes 2097184 | tf_op jit(solution)/shard_map/all_to_all | solution.py:110
  448.2 5.4 all-to-all-start.12
  453.6 5.4 fusion.17
  459.1 4.6 multiply_convert_fusion.1
  474.4 9.5 %all-to-all-done.12 = bf16[128,8,1024]{2,1,0:T(8,128)(2,1)} async-done(((bf16[128,8,1024]{2,1,0:T(8,128)(2,1)}), bf16[128,8,1024]{2,1,0:T(8,128)(2,1)}, u32[]{:S(2)}, u32[]{:S(2)}) %all-to-all-start.12) | async-done | bytes 2097184 | tf_op jit(solution)/shard_map/all_to_all | solution.py:110
  483.9 5.8 all-to-all-start.15
  489.7 5.2 convolution_convert_fusion
  494.9 6.1 reshape.157
  500.9 18.9 %all-to-all-done.15 = f32[128,4,1024]{2,1,0:T(4,128)} async-done(((f32[128,4,1024]{2,1,0:T(4,128)}), f32[128,4,1024]{2,1,0:T(4,128)}, u32[]{:S(2)}, u32[]{:S(2)}) %all-to-all-start.15) | async-done | bytes 2097184 | tf_op jit(solution)/shard_map/all_to_all | solution.py:131
  519.8 5.5 all-to-all-start.5
  528.3 8.3 %fusion.5 = f32[128,8,1024]{2,1,0:T(8,128)} fusion(bf16[1536,512]{0,1:T(8,128)(2,1)} %get-tuple-element.10, bf16[1536,512]{0,1:T(8,128)(2,1)} %get-tuple-element.9, bf16[1024,1536]{1,0:T(8,128)(2,1)} %copy.48), kind=kOutput, calls=%fused_computation.22 | convolution fusion | flops 3227516928 | bytes 10485760 | tf_op jit(solution)/shard_map/dot_general | solution.py:36
  536.6 41.5 %all-to-all-done.5 = bf16[128,12,1024]{2,1,0:T(8,128)(2,1)} async-done(((bf16[128,12,1024]{2,1,0:T(8,128)(2,1)}), bf16[128,12,1024]{2,1,0:T(8,128)(2,1)}, u32[]{:S(2)}, u32[]{:S(2)}) %all-to-all-start.5) | async-done | bytes 3145760 | tf_op jit(solution)/shard_map/all_to_all | solution.py:116
  578.1 5.5 all-to-all-start.9
  591.5 44.9 %all-to-all-done.9 = f32[128,8,1024]{2,1,0:T(8,128)} async-done(((f32[128,8,1024]{2,1,0:T(8,128)}), f32[128,8,1024]{2,1,0:T(8,128)}, u32[]{:S(2)}, u32[]{:S(2)}) %all-to-all-start.9) | async-done | bytes 4194336 | tf_op jit(solution)/shard_map/all_to_all | solution.py:130
  636.4 4.7 all-to-all-start.16
  641.1 6.7 fusion.3
  647.8 4.4 copy.54
  652.2 19.4 %all-to-all-done.16 = f32[128,4,1024]{2,1,0:T(4,128)S(1)} async-done(((f32[128,4,1024]{2,1,0:T(4,128)}), f32[128,4,1024]{2,1,0:T(4,128)S(1)}, u32[]{:S(2)}, u32[]{:S(2)}) %all-to-all-start.16) | async-done | bytes 2097184 | tf_op jit(solution)/shard_map/all_to_all | solution.py:143
  672.9 5.9 all-to-all-start.10
  678.9 4.7 reshape.158
  683.6 5.3 gather_fusion
  692.8 5.6 fusion.32
  702.8 28.6 %all-to-all-done.10 = f32[128,8,1024]{2,1,0:T(8,128)} async-done(((f32[128,8,1024]{2,1,0:T(8,128)}), f32[128,8,1024]{2,1,0:T(8,128)}, u32[]{:S(2)}, u32[]{:S(2)}) %all-to-all-start.10) | async-done | bytes 4194336 | tf_op jit(solution)/shard_map/all_to_all | solution.py:142
  731.5 7.4 %fusion.12 = (bf16[1,1024,1024]{2,1,0:T(8,128)(2,1)}, bf16[1,1024,1024]{2,1,0:T(8,128)(2,1)}, bf16[1,1024,1024]{2,1,0:T(8,128)(2,1)}) fusion(f32[128,8,1024]{2,1,0:T(8,128)} %all-to-all-done.10, bf16[128,8,1024]{2,1,0:T(8,128)(2,1)} %all-to-all-done.12, bf16[128,8,1024]{2,1,0:T(8,128)(2,1)S(1)} %copy-done.8, bf16[128,8,1024]{2,1,0:T(8,128)(2,1)} %all-to-all-done.2), kind=kLoop, calls=%fused_computation.34 | loop fusion | flops 17825792 | bytes 16777216 | tf_op jit(solution)/shard_map/reshape | solution.py:152
  (90 shorter events, 76.5 us)
Async XLA Ops:
  0.6 265.3 %copy-start = (bf16[128,1024]{1,0:T(8,128)(2,1)S(1)}, bf16[128,1024]{1,0:T(8,128)(2,1)}, u32[]{:S(2)}) copy-start(bf16[128,1024]{1,0:T(8,128)(2,1)} %param.16) | copy-start | bytes 786436
  0.6 13.9 %copy-start.15 = (bf16[1,512,1024]{2,1,0:T(8,128)(2,1)S(1)}, bf16[1,512,1024]{2,1,0:T(8,128)(2,1)}, u32[]{:S(2)}) copy-start(bf16[1,512,1024]{2,1,0:T(8,128)(2,1)} %param.25) | copy-start | bytes 3145732
  3.0 30.8 %all-to-all-start.3 = ((bf16[128,4,1024]{2,1,0:T(4,128)(2,1)}), bf16[128,4,1024]{2,1,0:T(4,128)(2,1)S(1)}, u32[]{:S(2)}, u32[]{:S(2)}) async-start(bf16[128,4,1024]{2,1,0:T(4,128)(2,1)} %reshape.155), calls=%async_computation.3 | async-start | bytes 2097152 | tf_op jit(solution)/shard_map/all_to_all | solution.py:81
  33.9 47.7 %copy-start.9 = (bf16[128,4,1024]{2,1,0:T(4,128)(2,1)}, bf16[128,4,1024]{2,1,0:T(4,128)(2,1)S(1)}, u32[]{:S(2)}) copy-start(bf16[128,4,1024]{2,1,0:T(4,128)(2,1)S(1)} %all-to-all-done.3) | copy-start | bytes 3145732
  33.9 23.8 %all-to-all-start.13 = ((bf16[128,4,1024]{2,1,0:T(4,128)(2,1)}), bf16[128,4,1024]{2,1,0:T(4,128)(2,1)S(1)}, u32[]{:S(2)}, u32[]{:S(2)}) async-start(bf16[128,4,1024]{2,1,0:T(4,128)(2,1)} %reshape.164), calls=%async_computation.13 | async-start | bytes 2097152 | tf_op jit(solution)/shard_map/all_to_all | solution.py:83
  57.6 59.1 %copy-start.10 = (bf16[128,4,1024]{2,1,0:T(4,128)(2,1)}, bf16[128,4,1024]{2,1,0:T(4,128)(2,1)S(1)}, u32[]{:S(2)}) copy-start(bf16[128,4,1024]{2,1,0:T(4,128)(2,1)S(1)} %all-to-all-done.13) | copy-start | bytes 3145732
  57.6 23.9 %copy-start.13 = (bf16[1,1024,1024]{2,1,0:T(8,128)(2,1)S(1)}, bf16[1,1024,1024]{2,1,0:T(8,128)(2,1)}, u32[]{:S(2)}) copy-start(bf16[1,1024,1024]{2,1,0:T(8,128)(2,1)} %param.22) | copy-start | bytes 6291460
  81.6 35.1 %copy-start.14 = (bf16[1,1024,1024]{2,1,0:T(8,128)(2,1)S(1)}, bf16[1,1024,1024]{2,1,0:T(8,128)(2,1)}, u32[]{:S(2)}) copy-start(bf16[1,1024,1024]{2,1,0:T(8,128)(2,1)} %param.24) | copy-start | bytes 6291460
  151.8 4.5 copy-start.20
  151.8 35.2 %all-to-all-start.11 = ((bf16[128,8,1024]{2,1,0:T(8,128)(2,1)}), bf16[128,8,1024]{2,1,0:T(8,128)(2,1)S(1)}, u32[]{:S(2)}, u32[]{:S(2)}) async-start(bf16[128,8,1024]{2,1,0:T(8,128)(2,1)} %bitcast.59), calls=%async_computation.11 | async-start | bytes 4194304 | tf_op jit(solution)/shard_map/all_to_all | solution.py:84
  186.9 24.9 %copy-start.3 = (bf16[128,8,1024]{2,1,0:T(8,128)(2,1)}, bf16[128,8,1024]{2,1,0:T(8,128)(2,1)S(1)}, u32[]{:S(2)}) copy-start(bf16[128,8,1024]{2,1,0:T(8,128)(2,1)S(1)} %all-to-all-done.11) | copy-start | bytes 6291460
  186.9 29.2 %copy-start.18 = (s32[128,8]{0,1:T(8,128)S(1)}, s32[128,8]{0,1:T(8,128)}, u32[]{:S(2)}) copy-start(s32[128,8]{0,1:T(8,128)} %param.18) | copy-start | bytes 12292
  186.9 29.8 %copy-start.19 = (f32[128,8]{0,1:T(8,128)S(1)}, f32[128,8]{0,1:T(8,128)}, u32[]{:S(2)}) copy-start(f32[128,8]{0,1:T(8,128)} %param.19) | copy-start | bytes 12292
  211.8 23.8 %all-to-all-start.14 = ((bf16[128,4,1024]{2,1,0:T(4,128)(2,1)}), bf16[128,4,1024]{2,1,0:T(4,128)(2,1)S(1)}, u32[]{:S(2)}, u32[]{:S(2)}) async-start(bf16[128,4,1024]{2,1,0:T(4,128)(2,1)} %get-tuple-element.19), calls=%async_computation.14 | async-start | bytes 2097152 | tf_op jit(solution)/shard_map/all_to_all | solution.py:110
  235.6 6.3 copy-start.11
  235.6 6.3 copy-start.17
  235.6 24.9 %all-to-all-start.4 = ((bf16[128,4,1024]{2,1,0:T(4,128)(2,1)}), bf16[128,4,1024]{2,1,0:T(4,128)(2,1)}, u32[]{:S(2)}, u32[]{:S(2)}) async-start(bf16[128,4,1024]{2,1,0:T(4,128)(2,1)} %get-tuple-element.20), calls=%async_computation.4 | async-start | bytes 2097152 | tf_op jit(solution)/shard_map/all_to_all | solution.py:110
  260.5 58.2 %all-to-all-start.8 = ((bf16[128,12,1024]{2,1,0:T(8,128)(2,1)}), bf16[128,12,1024]{2,1,0:T(8,128)(2,1)}, u32[]{:S(2)}, u32[]{:S(2)}) async-start(bf16[128,12,1024]{2,1,0:T(8,128)(2,1)} %reshape.160), calls=%async_computation.8 | async-start | bytes 8388608 | tf_op jit(solution)/shard_map/all_to_all | solution.py:104
  275.0 49.2 %copy-start.5 = (bf16[128,8,1024]{2,1,0:T(8,128)(2,1)S(1)}, bf16[128,8,1024]{2,1,0:T(8,128)(2,1)}, u32[]{:S(2)}) copy-start(bf16[128,8,1024]{2,1,0:T(8,128)(2,1)} %all_to_all.96) | copy-start | bytes 6291460
  318.7 58.3 %all-to-all-start = ((bf16[128,12,1024]{2,1,0:T(8,128)(2,1)}), bf16[128,12,1024]{2,1,0:T(8,128)(2,1)}, u32[]{:S(2)}, u32[]{:S(2)}) async-start(bf16[128,12,1024]{2,1,0:T(8,128)(2,1)} %reshape.151), calls=%async_computation | async-start | bytes 8388608 | tf_op jit(solution)/shard_map/all_to_all | solution.py:103
  326.2 3.7 copy-start.4
  412.4 35.7 %all-to-all-start.2 = ((bf16[128,8,1024]{2,1,0:T(8,128)(2,1)}), bf16[128,8,1024]{2,1,0:T(8,128)(2,1)}, u32[]{:S(2)}, u32[]{:S(2)}) async-start(bf16[128,8,1024]{2,1,0:T(8,128)(2,1)} %get-tuple-element.23), calls=%async_computation.2 | async-start | bytes 4194304 | tf_op jit(solution)/shard_map/all_to_all | solution.py:110
  448.2 35.7 %all-to-all-start.12 = ((bf16[128,8,1024]{2,1,0:T(8,128)(2,1)}), bf16[128,8,1024]{2,1,0:T(8,128)(2,1)}, u32[]{:S(2)}, u32[]{:S(2)}) async-start(bf16[128,8,1024]{2,1,0:T(8,128)(2,1)} %get-tuple-element.22), calls=%async_computation.12 | async-start | bytes 4194304 | tf_op jit(solution)/shard_map/all_to_all | solution.py:110
  453.6 5.5 copy-start.12
  453.6 5.5 copy-start.16
  483.9 35.9 %all-to-all-start.15 = ((f32[128,4,1024]{2,1,0:T(4,128)}), f32[128,4,1024]{2,1,0:T(4,128)}, u32[]{:S(2)}, u32[]{:S(2)}) async-start(f32[128,4,1024]{2,1,0:T(4,128)} %copy.56), calls=%async_computation.15 | async-start | bytes 4194304 | tf_op jit(solution)/shard_map/all_to_all | solution.py:131
  519.8 58.3 %all-to-all-start.5 = ((bf16[128,12,1024]{2,1,0:T(8,128)(2,1)}), bf16[128,12,1024]{2,1,0:T(8,128)(2,1)}, u32[]{:S(2)}, u32[]{:S(2)}) async-start(bf16[128,12,1024]{2,1,0:T(8,128)(2,1)} %reshape.157), calls=%async_computation.5 | async-start | bytes 8388608 | tf_op jit(solution)/shard_map/all_to_all | solution.py:116
  536.6 47.0 %copy-start.2 = (s32[128]{0:T(128)S(1)}, s32[128]{0:T(128)}, u32[]{:S(2)}) copy-start(s32[128]{0:T(128)} %param.20) | copy-start | bytes 1540
  578.1 58.3 %all-to-all-start.9 = ((f32[128,8,1024]{2,1,0:T(8,128)}), f32[128,8,1024]{2,1,0:T(8,128)}, u32[]{:S(2)}, u32[]{:S(2)}) async-start(f32[128,8,1024]{2,1,0:T(8,128)} %fusion.5), calls=%async_computation.9 | async-start | bytes 8388608 | tf_op jit(solution)/shard_map/all_to_all | solution.py:130
  636.4 35.2 %all-to-all-start.16 = ((f32[128,4,1024]{2,1,0:T(4,128)}), f32[128,4,1024]{2,1,0:T(4,128)S(1)}, u32[]{:S(2)}, u32[]{:S(2)}) async-start(f32[128,4,1024]{2,1,0:T(4,128)} %copy.58), calls=%async_computation.16 | async-start | bytes 4194304 | tf_op jit(solution)/shard_map/all_to_all | solution.py:143
  671.6 1.3 copy-start.6
  672.9 58.5 %all-to-all-start.10 = ((f32[128,8,1024]{2,1,0:T(8,128)}), f32[128,8,1024]{2,1,0:T(8,128)}, u32[]{:S(2)}, u32[]{:S(2)}) async-start(f32[128,8,1024]{2,1,0:T(8,128)} %copy.54), calls=%async_computation.10 | async-start | bytes 8388608 | tf_op jit(solution)/shard_map/all_to_all | solution.py:142
  689.0 3.8 copy-start.7
  699.5 32.0 %copy-start.8 = (bf16[128,8,1024]{2,1,0:T(8,128)(2,1)S(1)}, bf16[128,8,1024]{2,1,0:T(8,128)(2,1)}, u32[]{:S(2)}) copy-start(bf16[128,8,1024]{2,1,0:T(8,128)(2,1)} %all_to_all.99) | copy-start | bytes 6291460
  731.5 7.4 %copy-start.1 = (bf16[128,1024]{1,0:T(8,128)(2,1)S(1)}, bf16[128,1024]{1,0:T(8,128)(2,1)}, u32[]{:S(2)}) copy-start(bf16[128,1024]{1,0:T(8,128)(2,1)} %param.16) | copy-start | bytes 786436
where the time goes:
time: 749 us; the launch traced here: 739 us
  waiting for transfers between devices  337 us (45%)
  blocking collectives  154 us (21%)
  local copies, waits for them, and re-layouts  94.3 us (13%)
  starting transfers between devices  79.7 us (11%)
  matrix products  38.3 us (5%)
  other arithmetic  33.9 us (5%)
    all_to_all x2, blocking collectives, shards(): lax.all_to_all(for_sending(chosen), 'ep', split_axis=0, concat_axis=0, ti...  60.3 us
    all_to_all x4, waiting for transfers between devices, shards(): lax.all_to_all(for_sending(chosen), 'ep', split_axis=0, concat_axis=0, ti...  46.8 us
    all_to_all x1, waiting for transfers between devices, shards(): lax.all_to_all(split_up(grad_gate_up), 'ep', split_axis=0, concat_axis=0,...  44.9 us
    all_to_all x1, waiting for transfers between devices, shards(): lax.all_to_all(send_dy, 'ep', split_axis=0, concat_axis=0, tiled=True)  43.7 us
    all_to_all x1, waiting for transfers between devices, shards(): lax.all_to_all(output.reshape(n_slots, capacity, model_width), 'ep', spli...  41.5 us
    all_to_all x1, waiting for transfers between devices, shards(): lax.all_to_all(send_x, 'ep', split_axis=0, concat_axis=0, tiled=True)  40.5 us
    all_to_all x1, blocking collectives, shards(): lax.all_to_all(split_up(gate_up_weight), 'ep', split_axis=0, concat_axis=...  35.1 us
    all_to_all x1, blocking collectives, shards(): lax.all_to_all(split_up(first_gate_up), 'ep', split_axis=0, concat_axis=0...  35 us
  transfers between devices with their start and end apart: 14, of which 14 were waited for; matrix products, arithmetic and copies ran while one was open for 21% of the time, Pallas kernels for 0%

commit v1 on v0

v1 whole, which is shorter than its diff:
```python
import jax
import jax.numpy as jnp
from jax import lax
from jax.sharding import PartitionSpec as P

N = 128
CAP = 12
BF = jnp.bfloat16
F32 = jnp.float32


def exchange(x):
    return lax.all_to_all(x, "ep", split_axis=0, concat_axis=0, tiled=True)


def pack(gate_up, down):
    a = gate_up.reshape(32, 32, 4, 256).transpose(0, 2, 1, 3).reshape(N, 32, 256)
    b = down.reshape(32, 16, 4, 256).transpose(0, 2, 1, 3).reshape(N, 16, 256)
    return jnp.concatenate([a, b], axis=1)


def unpack(pieces):
    a = pieces[:, :32].reshape(32, 4, 32, 256).transpose(0, 2, 1, 3).reshape(1024, 1024)
    b = pieces[:, 32:48].reshape(32, 4, 16, 256).transpose(0, 2, 1, 3).reshape(512, 1024)
    return a, b


def shards(
    tokens,
    cotangent,
    routes,
    gate_weights,
    old_experts,
    source,
    gate_up_weight,
    down_weight,
    first_gate_up,
    first_down,
    second_gate_up,
    second_down,
):
    w_pieces = exchange(pack(gate_up_weight[0], down_weight[0]))

    slots = jnp.arange(N, dtype=jnp.int32)
    named = routes[:, :, None] == slots
    hit = jnp.any(named, axis=1)
    gate_of = jnp.sum(jnp.where(named, gate_weights[:, :, None], 0.0), axis=1)
    below = (slots[:, None] > slots[None, :]).astype(BF)
    row = jnp.dot(below, hit.astype(BF), preferred_element_type=F32)
    row = jnp.where(hit, row, -1.0)
    ranks = jnp.arange(CAP, dtype=F32)
    place = (row.T[:, None, :] == ranks[None, :, None]).astype(BF)
    place = place.reshape(N * CAP, N)
    place_gate = jnp.sum(
        jnp.where(row.T[:, None, :] == ranks[None, :, None], gate_of.T[:, None, :], 0.0), axis=2
    ).reshape(N * CAP, 1)
    send_x = jnp.dot(place, tokens, preferred_element_type=F32).astype(BF)
    send_c = jnp.dot(place, cotangent, preferred_element_type=F32)
    send_dy = (place_gate * send_c).astype(BF)
    send = jnp.concatenate(
        [send_x.reshape(N, CAP, 1024), send_dy.reshape(N, CAP, 1024)], axis=1
    )
    rows = exchange(send)
    rows_x = rows[:, :CAP].reshape(N * CAP, 1024)
    rows_dy = rows[:, CAP:].reshape(N * CAP, 1024)

    w_home = exchange(jnp.take(w_pieces, source, axis=0))
    gate_up, down = unpack(w_home)

    state = jnp.concatenate(
        [pack(first_gate_up[0], first_down[0]), pack(second_gate_up[0], second_down[0])], axis=1
    )
    state_pieces = exchange(state)

    pre = jnp.dot(rows_x, gate_up, preferred_element_type=F32)
    gate_pre = pre[:, :512]
    up = pre[:, 512:]
    sig = jax.nn.sigmoid(gate_pre)
    act = gate_pre * sig
    hidden = (act * up).astype(BF)
    out = jnp.dot(hidden, down, preferred_element_type=F32).astype(BF)
    d_hidden = jnp.dot(rows_dy, down.T, preferred_element_type=F32)
    d_gate = d_hidden * up * sig * (1.0 + gate_pre * (1.0 - sig))
    d_up = d_hidden * act
    d_pre = jnp.concatenate([d_gate, d_up], axis=1).astype(BF)
    grad_gu = jnp.dot(rows_x.T, d_pre, preferred_element_type=F32).astype(BF)
    grad_dn = jnp.dot(hidden.T, rows_dy, preferred_element_type=F32).astype(BF)

    back = exchange(
        jnp.concatenate(
            [
                out.reshape(N, CAP, 4, 256).transpose(0, 2, 1, 3).reshape(N, 48, 256),
                pack(grad_gu, grad_dn),
            ],
            axis=1,
        )
    )
    returned = back[:, :48].reshape(N, 4, CAP, 256).transpose(0, 2, 1, 3).reshape(N * CAP, 1024)
    grads = back[:, 48:]

    new_expert = old_experts[source]
    same = (new_expert[:, None] == new_expert[None, :]).astype(BF)
    total = jnp.einsum("sr,rjc->sjc", same, grads, preferred_element_type=F32)
    chosen = jnp.take(state_pieces, source, axis=0)
    first_new = (0.9 * chosen[:, :48].astype(F32) + 0.1 * total).astype(BF)
    second_new = (0.95 * chosen[:, 48:].astype(F32) + 0.05 * total * total).astype(BF)
    final = exchange(jnp.concatenate([first_new, second_new], axis=1))

    gate_hi = place_gate.astype(BF)
    gate_lo = (place_gate - gate_hi.astype(F32)).astype(BF)
    combine = jnp.concatenate([place * gate_hi, place * gate_lo], axis=1)
    mixed = lax.dot_general(
        combine, returned, (((0,), (0,)), ((), ())), preferred_element_type=F32
    )
    layer_out = (mixed[:N] + mixed[N:]).astype(BF)

    m_gu, m_dn = unpack(final[:, :48])
    q_gu, q_dn = unpack(final[:, 48:])

    def step(w, m, q):
        return (
            w.astype(F32) - 0.01 * m.astype(F32) / (jnp.sqrt(q.astype(F32)) + 1e-8)
        ).astype(BF)

    return (
        layer_out,
        step(gate_up, m_gu, q_gu)[None],
        step(down, m_dn, q_dn)[None],
        m_gu[None],
        m_dn[None],
        q_gu[None],
        q_dn[None],
    )


def solution(mesh):
    tok = P("ep", None)
    slot = P("ep", None, None)
    return jax.shard_map(
        shards,
        mesh=mesh,
        in_specs=(tok,) * 4 + (P(), P()) + (slot,) * 6,
        out_specs=(tok,) + (slot,) * 6,
        check_vma=False,
    )
```

time: 749 us -> 536 us (0.72)
  blocking collectives: 154 us -> 0 us
  waiting for transfers between devices: 337 us -> 211 us
  local copies, waits for them, and re-layouts: 94.3 us -> 187 us
  starting transfers between devices: 79.7 us -> 46.1 us
  other arithmetic: 33.9 us -> 46.8 us
    all_to_all x5 -> x0, blocking collectives: 154 us -> none  [the longest x2 60.3 us: shards(): lax.all_to_all(for_sending(chosen), 'ep', split_axis=0, concat_axis=0, ti...]
    all_to_all x14 -> x6, waiting for transfers between devices: 337 us -> 211 us  [exchange(): return lax.all_to_all(x, 'ep', split_axis=0, concat_axis=0, tiled=True)]
    all_to_all x14 -> x6, starting transfers between devices: 79.7 us -> 46.1 us  [exchange(): return lax.all_to_all(x, 'ep', split_axis=0, concat_axis=0, tiled=True)]
    reshape x14 -> x19, local copies, waits for them, and re-layouts: 45 us -> 75.8 us  [the longest x4 16.8 us: unpack(): pieces[:, :32].reshape(32, 4, 32, 256).transpose(0, 2, 1, 3)]
    transpose x0 -> x12, local copies, waits for them, and re-layouts: none -> 22.8 us  [the longest x4 10 us: pack(): gate_up.reshape(32, 32, 4, 256).transpose(0, 2, 1, 3).reshape(N, 32, 256)]
    slice x0 -> x6, local copies, waits for them, and re-layouts: none -> 21.8 us  [the longest x1 6.86 us: shards(): rows_dy = rows[:, CAP:].reshape(N * CAP, 1024)]
    concatenate x0 -> x5, other arithmetic: none -> 19.8 us  [the longest x1 8.73 us: shards(): jnp.concatenate([send_x.reshape(N, CAP, 1024), send_dy.reshape(N, CAP, 10...]
    another operation x3 -> x6, local copies, waits for them, and re-layouts: 0.11 us -> 19.5 us  [the longest x3 12.3 us: pack(): gate_up.reshape(32, 32, 4, 256).transpose(0, 2, 1, 3).reshape(N, 32, 256)]
  transfers between devices with their start and end apart: 14 -> 6, of which waited for: 14 -> 5; matrix products, arithmetic and copies ran while one was open for 21% -> 37% of each run, Pallas kernels for 0% -> 0%
where the time goes in v1:
time: 536 us; the launch traced here: 526 us
  waiting for transfers between devices  211 us (39%)
  local copies, waits for them, and re-layouts  187 us (35%)
  other arithmetic  46.8 us (9%)
  starting transfers between devices  46.1 us (9%)
  matrix products  32.4 us (6%)
    all_to_all x6, waiting for transfers between devices, exchange(): return lax.all_to_all(x, 'ep', split_axis=0, concat_axis=0, tiled=True)  211 us
    all_to_all x6, starting transfers between devices, exchange(): return lax.all_to_all(x, 'ep', split_axis=0, concat_axis=0, tiled=True)  46.1 us
    reshape x4, local copies, waits for them, and re-layouts, unpack(): pieces[:, :32].reshape(32, 4, 32, 256).transpose(0, 2, 1, 3)  16.8 us
    convert_element_type x4, local copies, waits for them, and re-layouts, step(): w.astype(F32) - 0.01 * m.astype(F32) / (jnp.sqrt(q.astype(F32)) + 1e-08)  15 us
    reshape x2, local copies, waits for them, and re-layouts, pack(): b = down.reshape(32, 16, 4, 256).transpose(0, 2, 1, 3).reshape(N, 16, 256)  14.4 us
    select_n x1, other arithmetic, shards(): chosen = jnp.take(state_pieces, source, axis=0)  12.7 us
    another operation x3, local copies, waits for them, and re-layouts, pack(): gate_up.reshape(32, 32, 4, 256).transpose(0, 2, 1, 3).reshape(N, 32, 256)  12.3 us
  transfers between devices with their start and end apart: 6, of which 5 were waited for; matrix products, arithmetic and copies ran while one was open for 37% of the time, Pallas kernels for 0%

profile of v1, /device:TPU:1, one launch (start us, length us, event | category | flops | bytes accessed | tf_op | source)
XLA Modules:
  0.0 525.6 jit_solution(16557546686443198455)
XLA Ops:
  2.8 3.3 reshape_squeeze.18
  8.4 11.9 %all-to-all-start.1 = ((bf16[128,48,256]{2,1,0:T(8,128)(2,1)}), bf16[128,48,256]{2,1,0:T(8,128)(2,1)}, u32[]{:S(2)}, u32[]{:S(2)}) async-start(bf16[128,48,256]{2,1,0:T(8,128)(2,1)} %pad_maximum_fusion.4), calls=%async_computation.1 | async-start | bytes 6291456 | tf_op jit(solution)/shard_map/all_to_all | solution.py:13
  32.6 8.7 %pad_maximum_fusion = bf16[128,24,1024]{2,1,0:T(8,128)(2,1)} fusion(bf16[128,12,1024]{2,1,0:T(8,128)(2,1)} %reshape.247, bf16[128,12,1024]{2,1,0:T(8,128)(2,1)} %reshape.246), kind=kLoop, calls=%fused_computation.6 | loop fusion | flops 12582912 | bytes 12582912 | tf_op jit(solution)/shard_map/concatenate | solution.py:60
  41.4 20.2 %all-to-all-done.1 = bf16[128,48,256]{2,1,0:T(8,128)(2,1)} async-done(((bf16[128,48,256]{2,1,0:T(8,128)(2,1)}), bf16[128,48,256]{2,1,0:T(8,128)(2,1)}, u32[]{:S(2)}, u32[]{:S(2)}) %all-to-all-start.1) | async-done | bytes 3145760 | tf_op jit(solution)/shard_map/all_to_all | solution.py:13
  61.6 5.7 %all-to-all-start = ((bf16[128,24,1024]{2,1,0:T(8,128)(2,1)}), bf16[128,24,1024]{2,1,0:T(8,128)(2,1)}, u32[]{:S(2)}, u32[]{:S(2)}) async-start(bf16[128,24,1024]{2,1,0:T(8,128)(2,1)} %pad_maximum_fusion), calls=%async_computation | async-start | bytes 12582912 | tf_op jit(solution)/shard_map/all_to_all | solution.py:13
  72.0 70.6 %all-to-all-done = bf16[128,24,1024]{2,1,0:T(8,128)(2,1)} async-done(((bf16[128,24,1024]{2,1,0:T(8,128)(2,1)}), bf16[128,24,1024]{2,1,0:T(8,128)(2,1)}, u32[]{:S(2)}, u32[]{:S(2)}) %all-to-all-start) | async-done | bytes 6291488 | tf_op jit(solution)/shard_map/all_to_all | solution.py:13
  142.7 6.0 %all-to-all-start.2 = ((bf16[128,48,256]{2,1,0:T(8,128)(2,1)}), bf16[128,48,256]{2,1,0:T(8,128)(2,1)S(1)}, u32[]{:S(2)}, u32[]{:S(2)}) async-start(bf16[128,48,256]{2,1,0:T(8,128)(2,1)} %broadcast_select_fusion), calls=%async_computation.2 | async-start | bytes 6291456 | tf_op jit(solution)/shard_map/all_to_all | solution.py:13
  153.7 4.5 reshape_squeeze.22
  158.2 3.4 copy.125
  166.7 4.5 reshape_squeeze.20
  173.9 3.1 pad_maximum_fusion.2
  177.1 13.0 %all-to-all-done.2 = bf16[128,48,256]{2,1,0:T(8,128)(2,1)S(1)} async-done(((bf16[128,48,256]{2,1,0:T(8,128)(2,1)}), bf16[128,48,256]{2,1,0:T(8,128)(2,1)S(1)}, u32[]{:S(2)}, u32[]{:S(2)}) %all-to-all-start.2) | async-done | bytes 3145760 | tf_op jit(solution)/shard_map/all_to_all | solution.py:13
  191.9 5.7 %all-to-all-start.4 = ((bf16[128,96,256]{2,1,0:T(8,128)(2,1)}), bf16[128,96,256]{2,1,0:T(8,128)(2,1)}, u32[]{:S(2)}, u32[]{:S(2)}) async-start(bf16[128,96,256]{2,1,0:T(8,128)(2,1)} %pad_maximum_fusion.2), calls=%async_computation.4 | async-start | bytes 12582912 | tf_op jit(solution)/shard_map/all_to_all | solution.py:13
  197.6 6.9 %fusion.28 = (bf16[128,12,1024]{2,1,0:T(8,128)(2,1)}, bf16[128,12,1024]{2,1,0:T(8,128)(2,1)}) fusion(bf16[128,24,1024]{2,1,0:T(8,128)(2,1)} %all-to-all-done), kind=kLoop, calls=%fused_computation.66 | loop fusion | bytes 12582912 | tf_op jit(solution)/shard_map/slice | solution.py:65
  204.4 6.2 %reshape.248 = bf16[1536,1024]{1,0:T(8,128)(2,1)} reshape(bf16[128,12,1024]{2,1,0:T(8,128)(2,1)} %get-tuple-element.23) | data formatting | bytes 6291456 | tf_op jit(solution)/shard_map/reshape | solution.py:64
  216.1 6.2 %reshape.257 = bf16[1536,1024]{1,0:T(8,128)(2,1)} reshape(bf16[128,12,1024]{2,1,0:T(8,128)(2,1)} %get-tuple-element.22) | data formatting | bytes 6291456 | tf_op jit(solution)/shard_map/reshape | solution.py:65
  225.2 3.7 fusion.29
  228.9 4.4 multiply_convert_fusion.2
  234.4 2.8 convolution_convert_fusion.2
  242.5 11.7 %reshape.261 = bf16[128,16,256]{2,0,1:T(8,128)(2,1)} reshape(bf16[32,4,16,256]{3,1,0,2:T(4,128)(2,1)} %copy.118) | data formatting | bytes 2097152 | tf_op jit(solution)/shard_map/reshape | solution.py:18
  254.2 7.6 %fusion.9 = bf16[1024,1024]{1,0:T(8,128)(2,1)} fusion(bf16[1536,1024]{1,0:T(8,128)(2,1)} %reshape.248, bf16[1536,512]{0,1:T(8,128)(2,1)} %get-tuple-element.14, bf16[1536,512]{0,1:T(8,128)(2,1)} %get-tuple-element.13), kind=kOutput, calls=%fused_computation.32 | convolution fusion | flops 3228565504 | bytes 8388608 | tf_op jit(solution)/shard_map/dot_general | solution.py:86
  261.8 4.5 reshape.258
  266.3 4.0 copy.117
  270.3 4.0 reshape.259
  274.3 5.2 convolution_convert_fusion
  279.4 6.2 %reshape.255 = bf16[128,12,4,256]{3,2,1,0:T(4,128)(2,1)} reshape(bf16[1536,1024]{1,0:T(8,128)(2,1)} %convolution_convert_fusion) | data formatting | bytes 6291456 | tf_op jit(solution)/shard_map/reshape | solution.py:92
  285.6 3.1 copy.116
  288.8 3.6 pad_maximum_fusion.1
  292.4 6.3 %copy.119 = bf16[128,96,256]{2,1,0:T(8,128)(2,1)} copy(bf16[128,96,256]{2,0,1:T(8,128)(2,1)S(1)} %pad_maximum_fusion.1) | data formatting | bytes 12582912 | tf_op jit(solution)/shard_map/concatenate | solution.py:90
  298.7 10.9 %all-to-all-start.3 = ((bf16[128,96,256]{2,1,0:T(8,128)(2,1)}), bf16[128,96,256]{2,1,0:T(8,128)(2,1)}, u32[]{:S(2)}, u32[]{:S(2)}) async-start(bf16[128,96,256]{2,1,0:T(8,128)(2,1)} %copy.119), calls=%async_computation.3 | async-start | bytes 12582912 | tf_op jit(solution)/shard_map/all_to_all | solution.py:13
  310.8 6.4 %gather_fusion.1 = bf16[128,96,256]{2,1,0:T(8,128)(2,1)} fusion(bf16[128,96,256]{2,1,0:T(8,128)(2,1)} %all-to-all-done.4, s32[1024]{0:T(1024)S(1)} %pad_clamp_fusion), kind=kCustom, calls=%fused_computation.1 | custom fusion | bytes 12583424 | tf_op jit(solution)/shard_map/jit(_take)/gather | solution.py:104
  317.2 12.7 %copy_select_fusion = bf16[128,96,256]{2,0,1:T(8,128)(2,1)} fusion(bf16[128,96,256]{2,1,0:T(8,128)(2,1)} %gather_fusion.1, pred[128]{0:T(512)(128)(4,1)S(1)} %compare_and_fusion), kind=kLoop, calls=%fused_computation.10 | loop fusion | flops 3145728 | bytes 12583040 | tf_op jit(solution)/shard_map/jit(_take)/select_n | solution.py:104
  329.9 54.8 %all-to-all-done.3 = bf16[128,96,256]{2,1,0:T(8,128)(2,1)} async-done(((bf16[128,96,256]{2,1,0:T(8,128)(2,1)}), bf16[128,96,256]{2,1,0:T(8,128)(2,1)}, u32[]{:S(2)}, u32[]{:S(2)}) %all-to-all-start.3) | async-done | bytes 6291488 | tf_op jit(solution)/shard_map/all_to_all | solution.py:13
  384.7 5.1 fusion.27
  389.9 4.7 add_convert_fusion
  397.1 6.2 %copy.129 = bf16[128,96,256]{2,1,0:T(8,128)(2,1)} copy(bf16[128,96,256]{2,0,1:T(8,128)(2,1)S(1)} %pad_maximum_fusion.3) | data formatting | bytes 12582912 | tf_op jit(solution)/shard_map/concatenate | solution.py:107
  403.3 5.9 %all-to-all-start.5 = ((bf16[128,96,256]{2,1,0:T(8,128)(2,1)}), bf16[128,96,256]{2,1,0:T(8,128)(2,1)}, u32[]{:S(2)}, u32[]{:S(2)}) async-start(bf16[128,96,256]{2,1,0:T(8,128)(2,1)} %copy.129), calls=%async_computation.5 | async-start | bytes 12582912 | tf_op jit(solution)/shard_map/all_to_all | solution.py:13
  410.2 4.0 copy.122
  416.0 5.8 %reshape.276 = f32[1,1024,1024]{2,1,0:T(8,128)} reshape(f32[32,32,4,256]{3,2,1,0:T(4,128)} %copy.122) | data formatting | bytes 8388608 | tf_op jit(solution)/shard_map/convert_element_type | solution.py:122
  421.8 3.4 reshape.277
  431.6 52.8 %all-to-all-done.5 = bf16[128,96,256]{2,1,0:T(8,128)(2,1)} async-done(((bf16[128,96,256]{2,1,0:T(8,128)(2,1)}), bf16[128,96,256]{2,1,0:T(8,128)(2,1)}, u32[]{:S(2)}, u32[]{:S(2)}) %all-to-all-start.5) | async-done | bytes 6291488 | tf_op jit(solution)/shard_map/all_to_all | solution.py:13
  484.4 4.0 fusion.26
  488.4 3.3 copy.149
  491.7 3.4 reshape.271
  495.1 5.7 %copy.150 = bf16[32,4,32,256]{3,1,2,0:T(4,128)(2,1)} copy(bf16[32,4,32,256]{3,2,1,0:T(8,128)(2,1)} %bitcast.93) | data formatting | bytes 4194304 | tf_op jit(solution)/shard_map/reshape | solution.py:23
  500.8 4.4 reshape.269
  511.2 3.1 copy.152
  517.0 6.3 %subtract_convert_fusion = bf16[1,1024,1024]{2,1,0:T(8,128)(2,1)} fusion(f32[1,1024,1024]{2,1,0:T(8,128)} %reshape.276, bf16[1,1024,1024]{2,1,0:T(8,128)(2,1)S(1)} %reshape.271, bf16[1,1024,1024]{2,1,0:T(8,128)(2,1)} %reshape.269), kind=kLoop, calls=%fused_computation.13 | loop fusion | flops 7340032 | bytes 10485760 | tf_op jit(solution)/shard_map/convert_element_type | solution.py:123
  (110 shorter events, 74.5 us)
Async XLA Ops:
  0.6 23.6 %copy-start = (bf16[128,1024]{1,0:T(8,128)(2,1)S(1)}, bf16[128,1024]{1,0:T(8,128)(2,1)}, u32[]{:S(2)}) copy-start(bf16[128,1024]{1,0:T(8,128)(2,1)} %param.13) | copy-start | bytes 786436
  8.4 11.9 %copy-start.23 = (f32[128,8]{0,1:T(8,128)S(1)}, f32[128,8]{0,1:T(8,128)}, u32[]{:S(2)}) copy-start(f32[128,8]{0,1:T(8,128)} %param.15) | copy-start | bytes 12292
  8.4 12.0 %copy-start.24 = (s32[128,8]{0,1:T(8,128)S(1)}, s32[128,8]{0,1:T(8,128)}, u32[]{:S(2)}) copy-start(s32[128,8]{0,1:T(8,128)} %param.14) | copy-start | bytes 12292
  8.4 53.1 %all-to-all-start.1 = ((bf16[128,48,256]{2,1,0:T(8,128)(2,1)}), bf16[128,48,256]{2,1,0:T(8,128)(2,1)}, u32[]{:S(2)}, u32[]{:S(2)}) async-start(bf16[128,48,256]{2,1,0:T(8,128)(2,1)} %pad_maximum_fusion.4), calls=%async_computation.1 | async-start | bytes 6291456 | tf_op jit(solution)/shard_map/all_to_all | solution.py:13
  23.6 0.7 copy-start.15
  25.2 2.8 copy-start.16
  41.4 25.9 %copy-start.25 = (s32[128]{0:T(128)S(1)}, s32[128]{0:T(128)}, u32[]{:S(2)}) copy-start(s32[128]{0:T(128)} %param.17) | copy-start | bytes 1540
  61.6 81.1 %all-to-all-start = ((bf16[128,24,1024]{2,1,0:T(8,128)(2,1)}), bf16[128,24,1024]{2,1,0:T(8,128)(2,1)}, u32[]{:S(2)}, u32[]{:S(2)}) async-start(bf16[128,24,1024]{2,1,0:T(8,128)(2,1)} %pad_maximum_fusion), calls=%async_computation | async-start | bytes 12582912 | tf_op jit(solution)/shard_map/all_to_all | solution.py:13
  142.7 47.5 %all-to-all-start.2 = ((bf16[128,48,256]{2,1,0:T(8,128)(2,1)}), bf16[128,48,256]{2,1,0:T(8,128)(2,1)S(1)}, u32[]{:S(2)}, u32[]{:S(2)}) async-start(bf16[128,48,256]{2,1,0:T(8,128)(2,1)} %broadcast_select_fusion), calls=%async_computation.2 | async-start | bytes 6291456 | tf_op jit(solution)/shard_map/all_to_all | solution.py:13
  171.1 2.2 copy-start.8
  171.1 2.5 copy-start.13
  171.1 2.8 copy-start.14
  190.1 1.8 copy-start.3
  191.9 106.8 %all-to-all-start.4 = ((bf16[128,96,256]{2,1,0:T(8,128)(2,1)}), bf16[128,96,256]{2,1,0:T(8,128)(2,1)}, u32[]{:S(2)}, u32[]{:S(2)}) async-start(bf16[128,96,256]{2,1,0:T(8,128)(2,1)} %pad_maximum_fusion.2), calls=%async_computation.4 | async-start | bytes 12582912 | tf_op jit(solution)/shard_map/all_to_all | solution.py:13
  222.3 2.3 copy-start.17
  222.3 2.9 copy-start.19
  224.5 4.3 copy-start.20
  225.2 3.7 copy-start.18
  233.3 1.1 copy-start.26
  285.6 3.1 copy-start.7
  285.6 3.1 copy-start.12
  298.7 10.9 %copy-start.2 = (s32[128]{0:T(128)S(1)}, s32[128]{0:T(128)}, u32[]{:S(2)}) copy-start(s32[128]{0:T(128)} %param.16) | copy-start | bytes 1540
  298.7 86.0 %all-to-all-start.3 = ((bf16[128,96,256]{2,1,0:T(8,128)(2,1)}), bf16[128,96,256]{2,1,0:T(8,128)(2,1)}, u32[]{:S(2)}, u32[]{:S(2)}) async-start(bf16[128,96,256]{2,1,0:T(8,128)(2,1)} %copy.119), calls=%async_computation.3 | async-start | bytes 12582912 | tf_op jit(solution)/shard_map/all_to_all | solution.py:13
  384.7 5.2 copy-start.9
  403.3 81.1 %all-to-all-start.5 = ((bf16[128,96,256]{2,1,0:T(8,128)(2,1)}), bf16[128,96,256]{2,1,0:T(8,128)(2,1)}, u32[]{:S(2)}, u32[]{:S(2)}) async-start(bf16[128,96,256]{2,1,0:T(8,128)(2,1)} %copy.129), calls=%async_computation.5 | async-start | bytes 12582912 | tf_op jit(solution)/shard_map/all_to_all | solution.py:13
  421.8 3.4 copy-start.4
  428.8 1.0 copy-start.21
  428.8 1.1 copy-start.22
  495.1 21.8 %copy-start.5 = (bf16[1,1024,1024]{2,1,0:T(8,128)(2,1)}, bf16[1,1024,1024]{2,1,0:T(8,128)(2,1)S(1)}, u32[]{:S(2)}) copy-start(bf16[1,1024,1024]{2,1,0:T(8,128)(2,1)S(1)} %reshape.271) | copy-start | bytes 6291460
  511.2 12.0 %copy-start.10 = (bf16[1,512,1024]{2,1,0:T(8,128)(2,1)}, bf16[1,512,1024]{2,1,0:T(8,128)(2,1)S(1)}, u32[]{:S(2)}) copy-start(bf16[1,512,1024]{2,1,0:T(8,128)(2,1)S(1)} %reshape.275) | copy-start | bytes 3145732
  516.9 6.3 %copy-start.6 = (f32[1,512,1024]{2,1,0:T(8,128)S(1)}, f32[1,512,1024]{2,1,0:T(8,128)}, u32[]{:S(2)}) copy-start(f32[1,512,1024]{2,1,0:T(8,128)} %reshape.277) | copy-start | bytes 6291460
  516.9 6.3 %copy-start.11 = (bf16[1,512,1024]{2,1,0:T(8,128)(2,1)S(1)}, bf16[1,512,1024]{2,1,0:T(8,128)(2,1)}, u32[]{:S(2)}) copy-start(bf16[1,512,1024]{2,1,0:T(8,128)(2,1)} %reshape.273) | copy-start | bytes 3145732
  516.9 8.3 %copy-start.1 = (bf16[128,1024]{1,0:T(8,128)(2,1)S(1)}, bf16[128,1024]{1,0:T(8,128)(2,1)}, u32[]{:S(2)}) copy-start(bf16[128,1024]{1,0:T(8,128)(2,1)} %param.13) | copy-start | bytes 786436

commit v2 on v1

v2 whole, which is shorter than its diff:
```python
import jax
import jax.numpy as jnp
from jax import lax
from jax.sharding import PartitionSpec as P
from jax.experimental import pallas as pl
from jax.experimental.pallas import tpu as pltpu

N = 128
CAP = 12
ROWS = N * CAP
BF = jnp.bfloat16
F32 = jnp.float32
MESH = pl.DeviceIdType.MESH

ORDER = (("x", "y", "z"), ("y", "z", "x"), ("z", "x", "y"))
BUF = (4, 4, 2, 16, 1024)


def coordinates():
    me = lax.axis_index("ep")
    return {"z": me // 32, "y": (me // 8) % 4, "x": (me // 2) % 4, "c": me % 2}


def device(at, **moved):
    q = {**at, **moved}
    return (q["z"] * 32 + q["y"] * 8 + q["x"] * 2 + q["c"],)


def cut(ref, rows, **kw):
    if "x" in kw:
        cols = pl.ds(pl.multiple_of(kw["x"] * 256, 256), 256)
    else:
        cols = slice(None)
    every = slice(None)
    row = every if rows is None else pl.ds(rows, 16)
    return ref.at[kw.get("z", every), kw.get("y", every), kw.get("c", every), row, cols]


def bounce_shape(stream, phase):
    size = {"z": 4, "y": 4, "c": 2, "x": 4}
    size[ORDER[stream][phase]] = None
    if phase == 0:
        size["c"] = None
    lead = tuple(size[a] for a in "zyc" if size[a])
    return lead + (16, 1024 if size["x"] else 256)


def enter(at):
    bar = pltpu.get_barrier_semaphore()
    pl.semaphore_signal(bar, inc=1, device_id=device(at, c=1 - at["c"]), device_id_type=MESH)
    for axis in "zyx":
        for d in (1, 2, 3):
            for dc in (0, 1):
                there = {axis: (at[axis] + d) % 4, "c": (at["c"] + dc) % 2}
                pl.semaphore_signal(
                    bar, inc=1, device_id=device(at, **there), device_id_type=MESH
                )
    pl.semaphore_wait(bar, 19)


class Exchanges:
    def __init__(self, at, stages, sends, receives, bounces, bounce_sems):
        self.at, self.stages = at, stages
        self.sends, self.receives = sends, receives
        self.bounces, self.bounce_sems = bounces, bounce_sems
        self.slots = len(bounces) // 9
        self.held = {}
        self.done = {g: 0 for g in stages}
        self.ids = {g: i for i, g in enumerate(stages)}

    def start(self, g, phase):
        at, i = self.at, self.ids[g]
        loads = []
        for s in range(3):
            if phase:
                self._arrived(g, s, phase - 1)
            (src, src_rows), (dst, dst_rows) = self.stages[g][s][phase : phase + 2]
            axis = ORDER[s][phase]
            mine = {axis: at[axis]}
            if phase == 0:
                mine["c"] = at["c"]
            used = {v for k, v in self.held.items() if k[1:] == (s, phase)}
            slot = min(set(range(self.slots)) - used)
            self.held[g, s, phase] = slot
            n = slot * 9 + s * 3 + phase
            load = pltpu.make_async_copy(
                cut(src, src_rows, **mine), self.bounces[n], self.bounce_sems.at[n]
            )
            load.start()
            loads.append((load, n, cut(dst, dst_rows, **mine), s))
        for d in (2, 1, 3, 0):
            for dc in (0, 1) if phase == 0 else (0,):
                if d == 0 and dc == 0:
                    continue
                for s in range(3):
                    (src, src_rows), (dst, dst_rows) = self.stages[g][s][phase : phase + 2]
                    axis = ORDER[s][phase]
                    mine = {axis: at[axis]}
                    there = {axis: (at[axis] + d) % 4}
                    if phase == 0:
                        mine["c"] = at["c"]
                        there["c"] = (at["c"] + dc) % 2
                    pltpu.make_async_remote_copy(
                        cut(src, src_rows, **there),
                        cut(dst, dst_rows, **mine),
                        self.sends.at[i, s, phase],
                        self.receives.at[i, s, phase],
                        device_id=device(at, **there),
                        device_id_type=MESH,
                    ).start()
        for load, n, dst, s in loads:
            load.wait()
            pltpu.make_async_copy(
                self.bounces[n], dst, self.receives.at[i, s, phase]
            ).start()

    def _arrived(self, g, s, phase):
        dst, rows = self.stages[g][s][phase + 1]
        whole = cut(dst, rows)
        pltpu.make_async_copy(whole, whole, self.receives.at[self.ids[g], s, phase]).wait()
        del self.held[g, s, phase]

    def finish(self, g):
        for s in range(3):
            self._arrived(g, s, 2)

    def drain(self):
        for g, i in self.ids.items():
            for s in range(3):
                for phase in range(3):
                    ref, rows = self.stages[g][s][phase + 1]
                    row = slice(None) if rows is None else pl.ds(rows, 16)
                    sent = ref.at[:, :, :, row, pl.ds(0, 768 if phase else 896)]
                    pltpu.make_async_copy(sent, sent, self.sends.at[i, s, phase]).wait()


def to_pieces(back, rows48, store):
    stacked = jnp.concatenate([rows48[:, q * 256 : q * 256 + 256] for q in range(4)], axis=0)
    moved = jnp.dot(back, stacked, preferred_element_type=F32).astype(BF)
    for s in range(3):
        store(s, moved[s * 64 : s * 64 + 64].reshape(4, 16, 256))


def from_pieces(there, refs, g, x):
    parts = [
        refs[s][g // 2, pl.ds(2 * (g % 2), 2), :, :, pl.ds(x * 256, 256)].reshape(64, 256)
        for s in range(3)
    ]
    return jnp.dot(
        there, jnp.concatenate(parts, axis=0), preferred_element_type=F32
    ).astype(BF)


def relayout(there, refs, out):
    def body(g, carry):
        for x in range(4):
            moved = from_pieces(there, refs, g, x)
            at = pl.multiple_of(x * 384 + g * 48, 16)
            for q in range(4):
                out[pl.ds(at, 48), q * 256 : q * 256 + 256] = moved[q * 48 : q * 48 + 48]
        return carry

    lax.fori_loop(0, 8, body, 0)


def piece_of(ref, table, is_x, i):
    full = ref[table[0, i], table[1, i], table[2, i]].astype(F32)
    return sum(full[:, x * 256 : x * 256 + 256] * is_x[x, i] for x in range(4))


def first_kernel(*refs):
    source, source_x = refs[:2]
    refs = refs[1:]
    (place, place_gate, there, back, tokens, cotangent) = refs[1:7]
    w_gu, w_dn, m_gu, m_dn, q_gu, q_dn = refs[7:13]
    (home_gu, home_dn) = refs[13:15]
    out_m, out_q, out_y = refs[15:18], refs[18:21], refs[21:24]
    out_ggu, out_gdn = refs[24:26]
    mids = refs[26:62]
    scratch = refs[62:]
    w_land, w_stage = scratch[0:3], scratch[3:6]
    x_send, c_send = scratch[6:9], scratch[9:12]
    x_land, c_land = scratch[12:15], scratch[15:18]
    gu, dn, xs, cs, hidden, d_pre = scratch[18:24]
    sends, receives, bounce_sems, copy_sem = scratch[24:28]
    bounces = scratch[28:]

    def mid(i):
        return [(mids[i * 6 + s], None) for s in range(3)], [
            (mids[i * 6 + 3 + s], None) for s in range(3)
        ]

    def raw(a, b):
        return [(a, 0), (a, 16), (b, None)]

    def plain(group):
        return [(r, None) for r in group]

    ends = {
        "w1": (raw(w_gu, w_dn), plain(w_land)),
        "x": (plain(x_send), plain(x_land)),
        "dy": (plain(c_send), plain(c_land)),
        "w2": (plain(w_stage), raw(gu, dn)),
        "m": (raw(m_gu, m_dn), plain(out_m)),
        "q": (raw(q_gu, q_dn), plain(out_q)),
    }
    stages = {}
    for i, (g, (first, last)) in enumerate(ends.items()):
        one, two = mid(i)
        stages[g] = [(first[s], one[s], two[s], last[s]) for s in range(3)]

    at = coordinates()
    enter(at)
    ex = Exchanges(at, stages, sends, receives, bounces, bounce_sems)

    def dispatch(rows, gate, out):
        def body(g, carry):
            for x in range(4):
                r = pl.ds(pl.multiple_of(x * 384 + g * 48, 16), 48)
                got = jnp.dot(place[r], rows[...], preferred_element_type=F32)
                if gate is not None:
                    got = got * gate[r]

                def store(s, value, x=x):
                    out[s][g // 2, pl.ds(2 * (g % 2), 2), :, :, x * 256 : x * 256 + 256] = (
                        value.reshape(2, 2, 16, 256)
                    )

                to_pieces(back[...], got.astype(BF), store)
            return carry

        lax.fori_loop(0, 8, body, 0)

    def select():
        def body(i, carry):
            z, y, c = i // 8, (i // 2) % 4, i % 2
            for x in range(4):
                slot = z * 32 + y * 8 + x * 2 + c
                for s in range(3):
                    w_stage[s][z, y, c, :, x * 256 : x * 256 + 256] = piece_of(
                        w_land[s], source, source_x, slot
                    ).astype(BF)
            return carry

        lax.fori_loop(0, 32, body, 0)

    ex.start("w1", 0)
    ex.start("m", 0)
    dispatch(tokens, None, x_send)
    ex.start("w1", 1)
    ex.start("x", 0)
    dispatch(cotangent, place_gate, c_send)
    ex.start("w1", 2)
    ex.start("dy", 0)
    ex.start("x", 1)
    ex.finish("w1")
    select()
    ex.start("w2", 0)
    ex.start("dy", 1)
    ex.start("w2", 1)
    ex.start("x", 2)
    ex.start("w2", 2)
    ex.start("dy", 2)
    ex.start("m", 1)
    ex.start("q", 0)
    ex.finish("x")
    relayout(there[...], x_land, xs)
    ex.finish("w2")
    keep_gu = pltpu.make_async_copy(gu, home_gu, copy_sem.at[0])
    keep_dn = pltpu.make_async_copy(dn, home_dn, copy_sem.at[1])
    keep_gu.start()
    keep_dn.start()
    ex.finish("dy")
    relayout(there[...], c_land, cs)
    ex.start("q", 1)

    def forward(b, carry):
        r = pl.ds(pl.multiple_of(b * 192, 16), 192)
        pre = jnp.zeros((192, 1024), F32)
        for k in range(4):
            pre += jnp.dot(
                xs[r, k * 256 : k * 256 + 256],
                gu[k].reshape(256, 1024),
                preferred_element_type=F32,
            )
        gate, up = pre[:, :512], pre[:, 512:]
        d_hid = jnp.concatenate(
            [
                lax.dot_general(
                    cs[r],
                    dn[k].reshape(128, 1024),
                    (((1,), (1,)), ((), ())),
                    preferred_element_type=F32,
                )
                for k in range(4)
            ],
            axis=1,
        )
        sig = jax.nn.sigmoid(gate)
        act = gate * sig
        h = (act * up).astype(BF)
        hidden[r] = h
        d_pre[r, 0:512] = (d_hid * up * sig * (1.0 + gate * (1.0 - sig))).astype(BF)
        d_pre[r, 512:1024] = (d_hid * act).astype(BF)
        y = jnp.zeros((192, 1024), F32)
        for k in range(4):
            y += jnp.dot(
                h[:, k * 128 : k * 128 + 128],
                dn[k].reshape(128, 1024),
                preferred_element_type=F32,
            )
        y = y.astype(BF)
        x, half = b // 2, b % 2
        cols = pl.ds(pl.multiple_of(x * 256, 256), 256)
        for j in range(4):
            g = half * 4 + j

            def store(s, value):
                out_y[s][g // 2, pl.ds(2 * (j % 2), 2), :, :, cols] = value.reshape(2, 2, 16, 256)

            to_pieces(back[...], y[j * 48 : j * 48 + 48], store)
        return carry

    lax.fori_loop(0, 8, forward, 0)
    ex.start("m", 2)
    ex.start("q", 2)
    for k in range(4):
        got = lax.dot_general(
            xs[:, k * 256 : k * 256 + 256],
            d_pre[...],
            (((0,), (0,)), ((), ())),
            preferred_element_type=F32,
        )
        out_ggu[k] = got.astype(BF).reshape(4, 2, 32, 1024)
        got = lax.dot_general(
            hidden[:, k * 128 : k * 128 + 128],
            cs[...],
            (((0,), (0,)), ((), ())),
            preferred_element_type=F32,
        )
        out_gdn[k] = got.astype(BF).reshape(4, 2, 16, 1024)
    ex.finish("m")
    ex.finish("q")
    ex.drain()
    keep_gu.wait()
    keep_dn.wait()


def second_kernel(*refs):
    source, source_x, order, order_x = refs[:4]
    refs = refs[2:]
    (last, keep, there, combine) = refs[2:6]
    g_gu, g_dn = refs[6:8]
    y_send, m_in, q_in = refs[8:11], refs[11:14], refs[14:17]
    layer_out = refs[17]
    new_m, new_q = refs[18:20], refs[20:22]
    mids = refs[22:46]
    scratch = refs[46:]
    g_land, y_land = scratch[0:3], scratch[3:6]
    m_old, q_old, m_send, q_send = (
        scratch[6:9],
        scratch[9:12],
        scratch[12:15],
        scratch[15:18],
    )
    sums, ys = scratch[18:20]
    sends, receives, bounce_sems, copy_sem = scratch[20:24]
    bounces = scratch[24:]

    def plain(group):
        return [(r, None) for r in group]

    def raw(a, b):
        return [(a, 0), (a, 16), (b, None)]

    ends = {
        "g": (raw(g_gu, g_dn), plain(g_land)),
        "y": (plain(y_send), plain(y_land)),
        "m": (plain(m_send), raw(*new_m)),
        "q": (plain(q_send), raw(*new_q)),
    }
    stages = {}
    for i, (g, (first, end)) in enumerate(ends.items()):
        stages[g] = [
            (first[s], (mids[i * 6 + s], None), (mids[i * 6 + 3 + s], None), end[s])
            for s in range(3)
        ]
    at = coordinates()
    enter(at)
    ex = Exchanges(at, stages, sends, receives, bounces, bounce_sems)
    ex.start("g", 0)
    ex.start("y", 0)
    fetch = [
        pltpu.make_async_copy(a, b, copy_sem.at[i])
        for i, (a, b) in enumerate(zip(m_in + q_in, m_old + q_old))
    ]
    for f in fetch:
        f.start()
    ex.start("g", 1)
    ex.start("y", 1)
    ex.start("g", 2)
    ex.finish("g")

    def running(i, acc):
        new = []
        for s in range(3):
            part = piece_of(g_land[s], order, order_x, i)
            new.append(acc[s] * keep[i] + part)
            sums[s, i] = new[s]
        return tuple(new)

    lax.fori_loop(0, N, running, (jnp.zeros((16, 256), F32),) * 3)
    ex.start("y", 2)
    for f in fetch:
        f.wait()

    def update(old, out, rule):
        def body(i, carry):
            z, y, c = i // 8, (i // 2) % 4, i % 2
            for x in range(4):
                slot = z * 32 + y * 8 + x * 2 + c
                e = last[slot]
                for s in range(3):
                    was = piece_of(old[s], source, source_x, slot)
                    out[s][z, y, c, :, x * 256 : x * 256 + 256] = rule(was, sums[s, e]).astype(BF)
            return carry

        lax.fori_loop(0, 32, body, 0)

    update(m_old, m_send, lambda was, t: 0.9 * was + 0.1 * t)
    ex.start("m", 0)
    update(q_old, q_send, lambda was, t: 0.95 * was + 0.05 * t * t)
    ex.start("q", 0)
    ex.start("m", 1)
    ex.finish("y")
    relayout(there[...], y_land, ys)
    mixed = lax.dot_general(
        combine[...], ys[...], (((1,), (0,)), ((), ())), preferred_element_type=F32
    )
    layer_out[...] = (mixed[:N] + mixed[N:]).astype(BF)
    ex.start("q", 1)
    ex.start("m", 2)
    ex.start("q", 2)
    ex.finish("m")
    ex.finish("q")
    ex.drain()


def shape(*dims, dtype=BF):
    return jax.ShapeDtypeStruct(dims, dtype)


def semaphores(groups, slots):
    dma = pltpu.SemaphoreType.DMA
    return [dma((groups, 3, 3)), dma((groups, 3, 3)), dma((slots * 9,)), dma((8,))]


def bounce_buffers(slots):
    return [
        pltpu.VMEM(bounce_shape(s, phase), BF)
        for _ in range(slots)
        for s in range(3)
        for phase in range(3)
    ]


def shards(
    tokens,
    cotangent,
    routes,
    gate_weights,
    old_experts,
    source,
    gate_up_weight,
    down_weight,
    first_gate_up,
    first_down,
    second_gate_up,
    second_down,
):
    seen = jnp.arange(N, dtype=jnp.int32)
    slots = (seen % 32) // 8 * 32 + (seen % 8) // 2 * 8 + seen // 32 * 2 + seen % 2
    named = routes[:, :, None] == slots
    hit = jnp.any(named, axis=1)
    gate_of = jnp.sum(jnp.where(named, gate_weights[:, :, None], 0.0), axis=1)
    below = (seen[:, None] > seen[None, :]).astype(BF)
    row = jnp.dot(below, hit.astype(BF), preferred_element_type=F32)
    row = jnp.where(hit, row, -1.0).T
    ranks = jnp.arange(CAP, dtype=F32)
    at_rank = row[:, None, :] == ranks[None, :, None]
    place = at_rank.astype(BF).reshape(ROWS, N)
    weighed = jnp.where(at_rank, gate_of.T[:, None, :], 0.0).reshape(ROWS, N)
    place_gate = jnp.sum(weighed, axis=1, keepdims=True)
    high = weighed.astype(BF)
    low = (weighed - high.astype(F32)).astype(BF)
    combine = jnp.concatenate([high, low], axis=1).T

    index = jnp.arange(192, dtype=jnp.int32)
    flat = index // 64 * 16 + index % 16
    where_to = flat // 12 * 48 + (index % 64) // 16 * 12 + flat % 12
    there = (index[:, None] == where_to[None, :]).astype(BF)
    back = there.T

    new_expert = old_experts[source]
    order = jnp.argsort(new_expert, stable=True).astype(jnp.int32)
    sorted_expert = new_expert[order]
    keep = jnp.concatenate(
        [jnp.zeros((1,), F32), (sorted_expert[1:] == sorted_expert[:-1]).astype(F32)]
    )
    last = jnp.sum((sorted_expert[None, :] <= new_expert[:, None]).astype(jnp.int32), axis=1) - 1

    def places(device):
        is_x = ((device // 2) % 4)[None, :] == jnp.arange(4)[:, None]
        lead = jnp.stack([device // 32, (device // 8) % 4, device % 2]).astype(jnp.int32)
        return lead, is_x.astype(F32)

    (source, source_x), (order, order_x) = places(source), places(order)
    gu_shape, dn_shape = (4, 4, 2, 32, 1024), BUF
    arrays = (
        gate_up_weight.reshape(gu_shape),
        down_weight.reshape(dn_shape),
        first_gate_up.reshape(gu_shape),
        first_down.reshape(dn_shape),
        second_gate_up.reshape(gu_shape),
        second_down.reshape(dn_shape),
    )
    smem = pl.BlockSpec(memory_space=pltpu.SMEM)
    vmem = pl.BlockSpec(memory_space=pltpu.VMEM)
    hbm = pl.BlockSpec(memory_space=pl.ANY)
    buf = shape(*BUF)
    mega = 1 << 20
    slots_a, slots_b = 3, 2
    outs = pl.pallas_call(
        first_kernel,
        out_shape=[shape(*gu_shape), buf] + [buf] * 9 + [shape(*gu_shape), buf] + [buf] * 36,
        in_specs=[smem] * 2 + [vmem] * 6 + [hbm] * 6,
        out_specs=[hbm] * 8 + [vmem] * 5 + [hbm] * 36,
        scratch_shapes=[pltpu.VMEM(BUF, BF)] * 18
        + [pltpu.VMEM(gu_shape, BF), pltpu.VMEM(BUF, BF)]
        + [pltpu.VMEM((ROWS, 1024), BF)] * 2
        + [pltpu.VMEM((ROWS, 512), BF), pltpu.VMEM((ROWS, 1024), BF)]
        + semaphores(6, slots_a)
        + bounce_buffers(slots_a),
        compiler_params=pltpu.CompilerParams(
            collective_id=0, has_side_effects=True, vmem_limit_bytes=62 * mega
        ),
    )(source, source_x, place, place_gate, there, back, tokens, cotangent, *arrays)
    home_gu, home_dn = outs[0], outs[1]
    m_pieces, q_pieces, y_pieces = outs[2:5], outs[5:8], outs[8:11]
    g_gu, g_dn = outs[11:13]

    outs = pl.pallas_call(
        second_kernel,
        out_shape=[shape(N, 1024)] + [shape(*gu_shape), buf] * 2 + [buf] * 24,
        in_specs=[smem] * 6 + [vmem] * 2 + [hbm] * 11,
        out_specs=[vmem] + [hbm] * 28,
        scratch_shapes=[pltpu.VMEM(BUF, BF)] * 18
        + [pltpu.VMEM((3, N, 16, 256), F32), pltpu.VMEM((ROWS, 1024), BF)]
        + semaphores(4, slots_b)
        + bounce_buffers(slots_b),
        compiler_params=pltpu.CompilerParams(
            collective_id=1, has_side_effects=True, vmem_limit_bytes=62 * mega
        ),
    )(
        source,
        source_x,
        order,
        order_x,
        last,
        keep,
        there,
        combine,
        g_gu,
        g_dn,
        *y_pieces,
        *m_pieces,
        *q_pieces,
    )
    layer_out, m_gu, m_dn, q_gu, q_dn = outs[:5]

    def step(w, m, q):
        return (
            w.astype(F32) - 0.01 * m.astype(F32) / (jnp.sqrt(q.astype(F32)) + 1e-8)
        ).astype(BF)

    up_shape, down_shape = (1, 1024, 1024), (1, 512, 1024)
    return (
        layer_out,
        step(home_gu, m_gu, q_gu).reshape(up_shape),
        step(home_dn, m_dn, q_dn).reshape(down_shape),
        m_gu.reshape(up_shape),
        m_dn.reshape(down_shape),
        q_gu.reshape(up_shape),
        q_dn.reshape(down_shape),
    )


def solution(mesh):
    tok = P("ep", None)
    slot = P("ep", None, None)
    return jax.shard_map(
        shards,
        mesh=mesh,
        in_specs=(tok,) * 4 + (P(), P()) + (slot,) * 6,
        out_specs=(tok,) + (slot,) * 6,
        check_vma=False,
    )
```

time: 536 us -> 408 us (0.76); the launches traced: 526 us -> 407 us
  Pallas kernels: 0 us -> 375 us
  waiting for transfers between devices: 211 us -> 0 us
  local copies, waits for them, and re-layouts: 187 us -> 13.8 us
  starting transfers between devices: 46.1 us -> 0 us
  matrix products: 32.4 us -> 0.18 us
  other arithmetic: 46.8 us -> 17.6 us
    pallas_call x0 -> x2, Pallas kernels: none -> 375 us  [the longest x1 225 us: shards(): pl.pallas_call(first_kernel, out_shape=[shape(*gu_shape), buf] + [buf] *...]
    all_to_all x6 -> x0, waiting for transfers between devices: 211 us -> none  [exchange(): return lax.all_to_all(x, 'ep', split_axis=0, concat_axis=0, tiled=True)]
    reshape x19 -> x0, local copies, waits for them, and re-layouts: 75.8 us -> none  [the longest x4 16.8 us: unpack(): pieces[:, :32].reshape(32, 4, 32, 256).transpose(0, 2, 1, 3)]
    all_to_all x6 -> x0, starting transfers between devices: 46.1 us -> none  [exchange(): return lax.all_to_all(x, 'ep', split_axis=0, concat_axis=0, tiled=True)]
    dot_general x9 -> x0, matrix products: 32.2 us -> none  [the longest x1 7.61 us: shards(): grad_gu = jnp.dot(rows_x.T, d_pre, preferred_element_type=F32).astype(BF)]
    transpose x12 -> x1, local copies, waits for them, and re-layouts: 22.8 us -> 0.09 us  [shards(): weighed = jnp.where(at_rank, gate_of.T[:, None, :], 0.0).reshape(ROWS, N)]
    slice x6 -> x0, local copies, waits for them, and re-layouts: 21.8 us -> none  [the longest x1 6.86 us: shards(): rows_dy = rows[:, CAP:].reshape(N * CAP, 1024)]
    another operation x6 -> x0, local copies, waits for them, and re-layouts: 19.5 us -> none  [the longest x3 12.3 us: pack(): gate_up.reshape(32, 32, 4, 256).transpose(0, 2, 1, 3).reshape(N, 32, 256)]
  transfers between devices with their start and end apart: 6 -> 0, of which waited for: 5 -> 0; matrix products, arithmetic and copies ran while one was open for 37% -> 0% of each run, Pallas kernels for 0% -> 0%
where the time goes in v2:
time: 408 us; the launch traced here: 407 us
  Pallas kernels  375 us (92%)
  other arithmetic  17.6 us (4%)
  local copies, waits for them, and re-layouts  13.8 us (3%)
    pallas_call x1, Pallas kernels, shards(): pl.pallas_call(first_kernel, out_shape=[shape(*gu_shape), buf] + [buf] *...  225 us
    pallas_call x1, Pallas kernels, shards(): pl.pallas_call(second_kernel, out_shape=[shape(N, 1024)] + [shape(*gu_sha...  150 us
    convert_element_type x2, other arithmetic, step(): return (w.astype(F32) - 0.01 * m.astype(F32) / (jnp.sqrt(q.astype(F32)) +...  8.8 us
    unnamed x23, local copies, waits for them, and re-layouts  8.16 us

profile of v2, /device:TPU:1, one launch (start us, length us, event | category | flops | bytes accessed | tf_op | source)
XLA Modules:
  0.0 407.2 jit_solution(2295763960784881912)
XLA Ops:
  0.6 0.0 copy-start
  0.6 0.7 add_select_fusion.1
  1.3 0.0 copy-done
  1.4 1.2 gather_fusion
  2.6 2.5 sort.17
  5.2 0.6 pad_add_fusion
  5.7 0.6 fusion.4
  6.3 0.8 copy.29
  7.1 0.3 compare_reduce_fusion
  7.4 0.1 copy.30
  7.5 0.2 convolution_select_fusion
  7.7 0.8 copy.32
  8.5 0.3 fusion
  8.8 0.1 copy.33
  8.9 0.4 select_reduce_fusion
  9.3 1.1 broadcast_in_dim.67.refs_3_
  10.4 0.1 eq.121
  10.5 0.1 eq.122
  10.6 0.3 copy.31
  10.9 0.1 eq.124
  11.0 0.1 fusion.24
  11.1 0.9 copy.35.refs_2_
  12.1 0.7 fusion.2
  12.8 224.7 %shard_map.171 = (bf16[4,4,2,32,1024]{4,3,2,1,0:T(8,128)(2,1)}, bf16[4,4,2,16,1024]{4,3,2,1,0:T(8,128)(2,1)}, bf16[4,4,2,16,1024]{4,3,2,1,0:T(8,128)(2,1)}, bf16...) custom-call(s32[3,128]{1,0:T(4,128)} %get-tuple-element.59.refs_0_, ...), custom_call_target="tpu_custom_call" | custom-call | tf_op jit(solution)/shard_map/pallas_call | solution.py:533
  237.5 0.1 broadcast_in_dim.62
  237.6 0.1 broadcast_in_dim.63
  237.6 0.3 copy.34
  237.9 0.1 select_convert_fusion
  238.0 0.1 subtract_convert_fusion.2
  238.1 0.9 maximum_bitcast_fusion.refs_7_
  239.1 1.2 gather_fusion.1
  240.3 0.2 convert_reduce_fusion
  240.5 0.5 broadcast_add_fusion.refs_4_
  241.0 0.1 slice_compare_fusion
  241.1 0.6 add_convert_fusion.refs_5_
  241.7 150.1 %shard_map.172 = (bf16[128,1024]{1,0:T(8,128)(2,1)}, bf16[4,4,2,32,1024]{4,3,2,1,0:T(8,128)(2,1)}, bf16[4,4,2,16,1024]{4,3,2,1,0:T(8,128)(2,1)}, bf16[4,4,2,32,1...) custom-call(s32[3,128]{1,0:T(4,128)} %get-tuple-element.59.refs_0_, ...), custom_call_target="tpu_custom_call" | custom-call | tf_op jit(solution)/shard_map/pallas_call | solution.py:552
  391.7 0.0 copy-done.6
  391.8 0.0 copy-start.2
  391.8 0.0 copy-start.3
  391.8 3.7 subtract_convert_fusion.1
  395.5 5.1 %subtract_convert_fusion = bf16[4,4,2,32,1024]{4,3,2,1,0:T(8,128)(2,1)} fusion(bf16[4,4,2,32,1024]{4,3,2,1,0:T(8,128)(2,1)S(1)} %copy-done.2, bf16[4,4,2,32,1024]{4,3,2,1,0:T(8,128)(2,1)S(1)} %copy-done.3, bf16[4,4,2,32,1024]{4,3,2,1,0:T(8,128)(2,1)} %get-tuple-element.39), kind=kLoop, calls=%fused_computation.2 | loop fusion | flops 8388608 | bytes 8388608 | tf_op jit(solution)/shard_map/convert_element_type | solution.py:584
  400.6 0.7 copy.43
  401.3 1.3 copy.44
  402.6 0.6 copy-done.5
  403.3 1.0 copy.45
  404.2 1.3 copy.46
  405.5 0.6 copy-done.4
  406.2 1.0 copy.47
  (16 shorter events, 0.1 us)
Async XLA Ops:
  0.6 0.7 copy-start
  241.7 150.1 %copy-start.6 = (bf16[4,4,2,16,1024]{4,3,2,1,0:T(8,128)(2,1)S(1)}, bf16[4,4,2,16,1024]{4,3,2,1,0:T(8,128)(2,1)}, u32[]{:S(2)}) copy-start(bf16[4,4,2,16,1024]{4,3,2,1,0:T(8,128)(2,1)} %get-tuple-element.42) | copy-start | bytes 3145732
  391.8 3.7 copy-start.2
  391.8 3.7 copy-start.3
  395.5 5.1 %copy-start.7 = (bf16[128,1024]{1,0:T(8,128)(2,1)S(1)}, bf16[128,1024]{1,0:T(8,128)(2,1)}, u32[]{:S(2)}) copy-start(bf16[128,1024]{1,0:T(8,128)(2,1)} %get-tuple-element.70) | copy-start | bytes 786436
  401.3 2.0 copy-start.5
  404.2 2.0 copy-start.4
  404.2 2.9 copy-start.1

commit v3 on v2

v3 whole, which is shorter than its diff:
```python
import jax
import jax.numpy as jnp
import numpy as np
from jax import lax
from jax.sharding import PartitionSpec as P
from jax.experimental import pallas as pl
from jax.experimental.pallas import tpu as pltpu

N = 128
CAP = 12
ROWS = N * CAP
BF = jnp.bfloat16
F32 = jnp.float32
MESH = pl.DeviceIdType.MESH

ORDER = (("x", "y", "z"), ("y", "z", "x"), ("z", "x", "y"))
BUF = (4, 4, 2, 16, 1024)


def coordinates():
    me = lax.axis_index("ep")
    return {"z": me // 32, "y": (me // 8) % 4, "x": (me // 2) % 4, "c": me % 2}


def device(at, **moved):
    q = {**at, **moved}
    return (q["z"] * 32 + q["y"] * 8 + q["x"] * 2 + q["c"],)


def cut(ref, rows, **kw):
    if "x" in kw:
        cols = pl.ds(pl.multiple_of(kw["x"] * 256, 256), 256)
    else:
        cols = slice(None)
    every = slice(None)
    row = every if rows is None else pl.ds(rows, 16)
    return ref.at[kw.get("z", every), kw.get("y", every), kw.get("c", every), row, cols]


def bounce_shape(stream, phase):
    size = {"z": 4, "y": 4, "c": 2, "x": 4}
    size[ORDER[stream][phase]] = None
    if phase == 0:
        size["c"] = None
    lead = tuple(size[a] for a in "zyc" if size[a])
    return lead + (16, 1024 if size["x"] else 256)


def enter(at):
    bar = pltpu.get_barrier_semaphore()
    pl.semaphore_signal(bar, inc=1, device_id=device(at, c=1 - at["c"]), device_id_type=MESH)
    for axis in "zyx":
        for d in (1, 2, 3):
            for dc in (0, 1):
                there = {axis: (at[axis] + d) % 4, "c": (at["c"] + dc) % 2}
                pl.semaphore_signal(
                    bar, inc=1, device_id=device(at, **there), device_id_type=MESH
                )
    pl.semaphore_wait(bar, 19)


class Exchanges:
    def __init__(self, at, stages, sends, receives, bounces, bounce_sems):
        self.at, self.stages = at, stages
        self.sends, self.receives = sends, receives
        self.bounces, self.bounce_sems = bounces, bounce_sems
        self.slots = len(bounces) // 9
        self.held = {}
        self.drained = set()
        self.ids = {g: i for i, g in enumerate(stages)}

    def start(self, g, phase):
        at, i = self.at, self.ids[g]
        loads = []
        if phase:
            for s in range(3):
                self._arrived(g, s, phase - 1)
        for s in range(3):
            (src, src_rows), (dst, dst_rows) = self.stages[g][s][phase : phase + 2]
            axis = ORDER[s][phase]
            mine = {axis: at[axis]}
            if phase == 0:
                mine["c"] = at["c"]
            used = {v for k, v in self.held.items() if k[1:] == (s, phase)}
            slot = min(set(range(self.slots)) - used)
            self.held[g, s, phase] = slot
            n = slot * 9 + s * 3 + phase
            load = pltpu.make_async_copy(
                cut(src, src_rows, **mine), self.bounces[n], self.bounce_sems.at[n]
            )
            load.start()
            loads.append((load, n, cut(dst, dst_rows, **mine), s))
        for d in (2, 1, 3, 0):
            for dc in (0, 1) if phase == 0 else (0,):
                if d == 0 and dc == 0:
                    continue
                for s in range(3):
                    (src, src_rows), (dst, dst_rows) = self.stages[g][s][phase : phase + 2]
                    axis = ORDER[s][phase]
                    mine = {axis: at[axis]}
                    there = {axis: (at[axis] + d) % 4}
                    if phase == 0:
                        mine["c"] = at["c"]
                        there["c"] = (at["c"] + dc) % 2
                    pltpu.make_async_remote_copy(
                        cut(src, src_rows, **there),
                        cut(dst, dst_rows, **mine),
                        self.sends.at[i, s, phase],
                        self.receives.at[i, s, phase],
                        device_id=device(at, **there),
                        device_id_type=MESH,
                    ).start()
        for load, n, dst, s in loads:
            load.wait()
            pltpu.make_async_copy(
                self.bounces[n], dst, self.receives.at[i, s, phase]
            ).start()

    def _arrived(self, g, s, phase):
        dst, rows = self.stages[g][s][phase + 1]
        whole = cut(dst, rows)
        pltpu.make_async_copy(whole, whole, self.receives.at[self.ids[g], s, phase]).wait()
        del self.held[g, s, phase]

    def finish(self, g):
        for s in range(3):
            self._arrived(g, s, 2)

    def sent(self, g, phase):
        if (g, phase) in self.drained:
            return
        self.drained.add((g, phase))
        for s in range(3):
            ref, rows = self.stages[g][s][phase + 1]
            row = slice(None) if rows is None else pl.ds(rows, 16)
            part = ref.at[:, :, :, row, pl.ds(0, 768 if phase else 896)]
            pltpu.make_async_copy(part, part, self.sends.at[self.ids[g], s, phase]).wait()

    def drain(self):
        for g in self.ids:
            for phase in range(3):
                self.sent(g, phase)


def to_pieces(back, rows48, store):
    stacked = jnp.concatenate([rows48[:, q * 256 : q * 256 + 256] for q in range(4)], axis=0)
    moved = jnp.dot(back, stacked, preferred_element_type=F32).astype(BF)
    for s in range(3):
        store(s, moved[s * 64 : s * 64 + 64].reshape(4, 16, 256))


def from_pieces(there, refs, g, x):
    parts = [
        refs[s][g // 2, pl.ds(2 * (g % 2), 2), :, :, pl.ds(x * 256, 256)].reshape(64, 256)
        for s in range(3)
    ]
    return jnp.dot(
        there, jnp.concatenate(parts, axis=0), preferred_element_type=F32
    ).astype(BF)


def relayout(there, refs, out):
    def body(g, carry):
        for x in range(4):
            moved = from_pieces(there, refs, g, x)
            at = pl.multiple_of(x * 384 + g * 48, 16)
            for q in range(4):
                out[pl.ds(at, 48), q * 256 : q * 256 + 256] = moved[q * 48 : q * 48 + 48]
        return carry

    lax.fori_loop(0, 8, body, 0)


def piece_of(ref, table, j):
    full = ref[table[0, j], table[1, j], table[2, j]].astype(F32)
    return sum(full[:, x * 256 : x * 256 + 256] * table[3 + x, j].astype(F32) for x in range(4))


def routing(routes, gates, place, weighed):
    lane = lax.broadcasted_iota(jnp.int32, (N, N), 1)
    line = lax.broadcasted_iota(jnp.int32, (N, N), 0)
    slot = ((lane >> 3) & 3) * 32 + ((lane >> 1) & 3) * 8 + (lane >> 5) * 2 + (lane & 1)
    hit = jnp.zeros((N, N), F32)
    gate = jnp.zeros((N, N), F32)
    for k in range(8):
        named = routes[:, k : k + 1] == slot
        hit = jnp.where(named, 1.0, hit)
        gate = jnp.where(named, gates[:, k : k + 1], gate)
    below = jnp.where(line > lane, 1.0, 0.0).astype(BF)
    row = jnp.dot(below, hit.astype(BF), preferred_element_type=F32)
    row = jnp.where(hit > 0.0, row, -1.0).T
    gate = gate.T
    high = gate.astype(BF)
    rest = gate - high.astype(F32)
    middle = rest.astype(BF)
    low = (rest - middle.astype(F32)).astype(BF)
    row = row.astype(BF)

    def body(b, carry):
        i = lax.broadcasted_iota(jnp.int32, (192, N), 0)
        first = (lax.broadcasted_iota(jnp.int32, (192, N), 1) - b * 16) * CAP
        spread = jnp.where((i >= first) & (i < first + CAP), 1.0, 0.0).astype(BF)
        rank = i.astype(F32)
        rank = rank - jnp.floor((rank + 0.5) * (1.0 / CAP)) * CAP

        def copies(v):
            return jnp.dot(spread, v, preferred_element_type=F32)

        here = copies(row) == rank
        r = pl.ds(pl.multiple_of(b * 192, 16), 192)
        place[r] = jnp.where(here, 1.0, 0.0).astype(BF)
        weighed[r] = jnp.where(here, copies(high) + copies(middle) + copies(low), 0.0)
        return carry

    lax.fori_loop(0, 8, body, 0)


def step_kernel(*refs):
    table, there, back, routes, gates, tokens, cotangent = refs[:7]
    w_gu, w_dn, m_gu, m_dn, q_gu, q_dn = refs[7:13]
    layer_out, home_gu, home_dn = refs[13:16]
    new_m, new_q = refs[16:18], refs[18:20]
    m_far, q_far = refs[20:23], refs[23:26]
    mids = refs[26:86]
    scratch = refs[86:]
    w_land, x_land, c_land, g_land, y_land = (scratch[i : i + 3] for i in range(0, 15, 3))
    w_stage, x_send, c_send = (scratch[i : i + 3] for i in range(15, 24, 3))
    gu, dn, g_gu, g_dn, xs, cs, hidden, d_pre, sums, place, weighed = scratch[24:35]
    sends, receives, bounce_sems, copy_sem = scratch[35:39]
    bounces = scratch[39:]
    y_send, m_send, q_send = x_send, w_stage, c_send
    m_old, q_old, ys = x_land, c_land, xs

    def raw(a, b):
        return [(a, 0), (a, 16), (b, None)]

    def plain(group):
        return [(r, None) for r in group]

    ends = {
        "w": (raw(w_gu, w_dn), plain(w_land)),
        "x": (plain(x_send), plain(x_land)),
        "c": (plain(c_send), plain(c_land)),
        "home": (plain(w_stage), raw(gu, dn)),
        "m": (raw(m_gu, m_dn), plain(m_far)),
        "q": (raw(q_gu, q_dn), plain(q_far)),
        "g": (raw(g_gu, g_dn), plain(g_land)),
        "y": (plain(y_send), plain(y_land)),
        "new_m": (plain(m_send), raw(*new_m)),
        "new_q": (plain(q_send), raw(*new_q)),
    }
    stages = {}
    for i, (g, (first, end)) in enumerate(ends.items()):
        stages[g] = [
            (first[s], (mids[i * 6 + s], None), (mids[i * 6 + 3 + s], None), end[s])
            for s in range(3)
        ]
    at = coordinates()
    enter(at)
    ex = Exchanges(at, stages, sends, receives, bounces, bounce_sems)

    def pair(g):
        return pl.ds(2 * (g % 2), 2)

    def dispatch(rows, scaled, out):
        def body(g, carry):
            for x in range(4):
                r = pl.ds(pl.multiple_of(x * 384 + g * 48, 16), 48)
                got = jnp.dot(place[r], rows[...], preferred_element_type=F32)
                if scaled:
                    got = got * jnp.sum(weighed[r], axis=1, keepdims=True)

                def store(s, value, x=x):
                    out[s][g // 2, pair(g), :, :, x * 256 : x * 256 + 256] = value.reshape(
                        2, 2, 16, 256
                    )

                to_pieces(back[...], got.astype(BF), store)
            return carry

        lax.fori_loop(0, 8, body, 0)

    def each_slot(do):
        def body(i, carry):
            z, y, c = i // 8, (i // 2) % 4, i % 2
            for x in range(4):
                for s in range(3):
                    do(s, (z, y, c, slice(None), slice(x * 256, x * 256 + 256)), i * 4 + x)
            return carry

        lax.fori_loop(0, 32, body, 0)

    def forward(b, carry):
        r = pl.ds(pl.multiple_of(b * 192, 16), 192)
        pre = jnp.zeros((192, 1024), F32)
        for k in range(4):
            pre += jnp.dot(
                xs[r, k * 256 : k * 256 + 256],
                gu[k].reshape(256, 1024),
                preferred_element_type=F32,
            )
        gate, up = pre[:, :512], pre[:, 512:]
        d_hid = jnp.concatenate(
            [
                lax.dot_general(
                    cs[r],
                    dn[k].reshape(128, 1024),
                    (((1,), (1,)), ((), ())),
                    preferred_element_type=F32,
                )
                for k in range(4)
            ],
            axis=1,
        )
        sig = jax.nn.sigmoid(gate)
        act = gate * sig
        h = (act * up).astype(BF)
        hidden[r] = h
        d_pre[r, 0:512] = (d_hid * up * sig * (1.0 + gate * (1.0 - sig))).astype(BF)
        d_pre[r, 512:1024] = (d_hid * act).astype(BF)
        y = jnp.zeros((192, 1024), F32)
        for k in range(4):
            y += jnp.dot(
                h[:, k * 128 : k * 128 + 128],
                dn[k].reshape(128, 1024),
                preferred_element_type=F32,
            )
        y = y.astype(BF)
        cols = pl.ds(pl.multiple_of(b // 2 * 256, 256), 256)
        for j in range(4):
            g = b % 2 * 4 + j

            def store(s, value):
                y_send[s][g // 2, pair(j), :, :, cols] = value.reshape(2, 2, 16, 256)

            to_pieces(back[...], y[j * 48 : j * 48 + 48], store)
        return carry

    ex.start("w", 0)
    ex.start("m", 0)
    routing(routes, gates, place, weighed)
    dispatch(tokens, False, x_send)
    ex.start("w", 1)
    ex.start("x", 0)
    dispatch(cotangent, True, c_send)
    ex.start("w", 2)
    ex.start("c", 0)
    ex.start("x", 1)
    ex.start("m", 1)
    ex.finish("w")

    def select(s, here, j):
        w_stage[s][here] = piece_of(w_land[s], table, j).astype(BF)

    each_slot(select)
    ex.start("home", 0)
    ex.start("c", 1)
    ex.start("x", 2)
    ex.start("home", 1)
    ex.start("c", 2)
    ex.start("q", 0)
    ex.start("home", 2)
    ex.start("m", 2)
    ex.finish("x")
    relayout(there[...], x_land, xs)
    ex.finish("c")
    relayout(there[...], c_land, cs)
    ex.start("q", 1)
    ex.finish("home")
    keep_gu = pltpu.make_async_copy(gu, home_gu, copy_sem.at[0])
    keep_dn = pltpu.make_async_copy(dn, home_dn, copy_sem.at[1])
    keep_gu.start()
    keep_dn.start()
    ex.sent("x", 0)
    lax.fori_loop(0, 8, forward, 0)
    ex.start("q", 2)
    for k in range(4):
        got = lax.dot_general(
            xs[:, k * 256 : k * 256 + 256],
            d_pre[...],
            (((0,), (0,)), ((), ())),
            preferred_element_type=F32,
        )
        g_gu[k] = got.astype(BF).reshape(4, 2, 32, 1024)
        got = lax.dot_general(
            hidden[:, k * 128 : k * 128 + 128],
            cs[...],
            (((0,), (0,)), ((), ())),
            preferred_element_type=F32,
        )
        g_dn[k] = got.astype(BF).reshape(4, 2, 16, 1024)
    ex.start("g", 0)
    ex.start("y", 0)
    ex.finish("m")
    ex.finish("q")
    fetch = [
        pltpu.make_async_copy(a, b, copy_sem.at[2 + i])
        for i, (a, b) in enumerate(zip(m_far + q_far, m_old + q_old))
    ]
    for f in fetch:
        f.start()
    ex.start("g", 1)
    ex.start("y", 1)
    ex.start("g", 2)
    for s in range(3):
        sums[s, N] = jnp.zeros((16, 256), F32)
    ex.finish("g")

    def add(s, here, j):
        sums[s, j] = g_land[s][here].astype(F32) + sums[s, table[7, j]]

    each_slot(add)
    ex.start("y", 2)
    for f in fetch:
        f.wait()
    ex.sent("home", 0)
    ex.sent("c", 0)

    def update_first(s, here, j):
        was = piece_of(m_old[s], table, j)
        m_send[s][here] = (0.9 * was + 0.1 * sums[s, table[8, j]]).astype(BF)

    def update_second(s, here, j):
        was = piece_of(q_old[s], table, j)
        total = sums[s, table[8, j]]
        q_send[s][here] = (0.95 * was + 0.05 * total * total).astype(BF)

    each_slot(update_first)
    ex.start("new_m", 0)
    each_slot(update_second)
    ex.start("new_q", 0)
    ex.start("new_m", 1)
    ex.finish("y")
    relayout(there[...], y_land, ys)
    ex.start("new_q", 1)
    ex.start("new_m", 2)
    high = weighed[...].astype(BF)
    low = (weighed[...] - high.astype(F32)).astype(BF)
    over_rows = (((0,), (0,)), ((), ()))
    mixed = lax.dot_general(high, ys[...], over_rows, preferred_element_type=F32)
    mixed += lax.dot_general(low, ys[...], over_rows, preferred_element_type=F32)
    layer_out[...] = mixed.astype(BF)
    ex.start("new_q", 2)
    ex.finish("new_m")
    ex.finish("new_q")
    ex.drain()
    keep_gu.wait()
    keep_dn.wait()


def weights_kernel(*refs):
    for i in range(2):
        w, m, q = (refs[3 * i + k] for k in range(3))
        new_w, new_m, new_q = (refs[6 + 3 * i + k] for k in range(3))
        rows = new_w.shape[1]
        first, second = m[...].reshape(rows, 1024), q[...].reshape(rows, 1024)
        weight = w[...].reshape(rows, 1024).astype(F32)
        change = 0.01 * first.astype(F32) / (jnp.sqrt(second.astype(F32)) + 1e-8)
        new_w[0] = (weight - change).astype(BF)
        new_m[0] = first
        new_q[0] = second


def shape(*dims, dtype=BF):
    return jax.ShapeDtypeStruct(dims, dtype)


def semaphores(groups, slots):
    dma = pltpu.SemaphoreType.DMA
    return [dma((groups, 3, 3)), dma((groups, 3, 3)), dma((slots * 9,)), dma((8,))]


def bounce_buffers(slots):
    return [
        pltpu.VMEM(bounce_shape(s, phase), BF)
        for _ in range(slots)
        for s in range(3)
        for phase in range(3)
    ]


def orders():
    i = np.arange(192)
    flat = i // 64 * 16 + i % 16
    where_to = flat // 12 * 48 + (i % 64) // 16 * 12 + flat % 12
    there = (i[:, None] == where_to[None, :]).astype(np.float32)
    return jnp.asarray(there, BF), jnp.asarray(there.T, BF)


def tables(old_experts, source):
    j = jnp.arange(N, dtype=jnp.int32)
    src = source.reshape(4, 4, 4, 2).transpose(0, 1, 3, 2).reshape(N)
    expert = jnp.sum(jnp.where(src[:, None] == j[None, :], old_experts[None, :], 0), axis=1)
    same = expert[:, None] == expert[None, :]
    before = jnp.max(jnp.where(same & (j[None, :] < j[:, None]), j[None, :], -1), axis=1)
    before = jnp.where(before < 0, N, before)
    last = jnp.max(jnp.where(same, j[None, :], -1), axis=1)
    x = (src // 2) % 4
    rows = [src // 32, (src // 8) % 4, src % 2] + [(x == k).astype(jnp.int32) for k in range(4)]
    return jnp.stack(rows + [before, last])


def shards(
    tokens,
    cotangent,
    routes,
    gate_weights,
    old_experts,
    source,
    gate_up_weight,
    down_weight,
    first_gate_up,
    first_down,
    second_gate_up,
    second_down,
):
    table = tables(old_experts, source)
    there, back = orders()
    gu_shape, dn_shape = (4, 4, 2, 32, 1024), BUF
    arrays = (
        gate_up_weight.reshape(gu_shape),
        down_weight.reshape(dn_shape),
        first_gate_up.reshape(gu_shape),
        first_down.reshape(dn_shape),
        second_gate_up.reshape(gu_shape),
        second_down.reshape(dn_shape),
    )
    smem = pl.BlockSpec(memory_space=pltpu.SMEM)
    vmem = pl.BlockSpec(memory_space=pltpu.VMEM)
    hbm = pl.BlockSpec(memory_space=pl.ANY)
    gu, buf = shape(*gu_shape), shape(*BUF)
    mega = 1 << 20
    slots = 4
    outs = pl.pallas_call(
        step_kernel,
        out_shape=[shape(N, 1024)] + [gu, buf] * 3 + [buf] * 66,
        in_specs=[smem] + [vmem] * 6 + [hbm] * 6,
        out_specs=[vmem] + [hbm] * 72,
        scratch_shapes=[pltpu.VMEM(BUF, BF)] * 24
        + [pltpu.VMEM(gu_shape, BF), pltpu.VMEM(BUF, BF)] * 2
        + [pltpu.VMEM((ROWS, 1024), BF)] * 2
        + [pltpu.VMEM((ROWS, 512), BF), pltpu.VMEM((ROWS, 1024), BF)]
        + [pltpu.VMEM((3, N + 1, 16, 256), F32)]
        + [pltpu.VMEM((ROWS, N), BF), pltpu.VMEM((ROWS, N), F32)]
        + semaphores(10, slots)
        + bounce_buffers(slots),
        compiler_params=pltpu.CompilerParams(
            collective_id=0, has_side_effects=True, vmem_limit_bytes=63 * mega
        ),
    )(table, there, back, routes, gate_weights, tokens, cotangent, *arrays)
    layer_out, home_gu, home_dn, m_gu, m_dn, q_gu, q_dn = outs[:7]

    def pieces(rows):
        return pl.BlockSpec((1, 2, 2, rows, 1024), lambda i: (i // 2, i % 2, 0, 0, 0))

    def whole(rows):
        return pl.BlockSpec((1, rows, 1024), lambda i: (0, i, 0))

    new = pl.pallas_call(
        weights_kernel,
        grid=(8,),
        out_shape=[shape(1, 1024, 1024)] * 3 + [shape(1, 512, 1024)] * 3,
        in_specs=[pieces(32)] * 3 + [pieces(16)] * 3,
        out_specs=[whole(128)] * 3 + [whole(64)] * 3,
        compiler_params=pltpu.CompilerParams(vmem_limit_bytes=32 * mega),
    )(home_gu, m_gu, q_gu, home_dn, m_dn, q_dn)
    return layer_out, new[0], new[3], new[1], new[4], new[2], new[5]


def solution(mesh):
    tok = P("ep", None)
    slot = P("ep", None, None)
    return jax.shard_map(
        shards,
        mesh=mesh,
        in_specs=(tok,) * 4 + (P(), P()) + (slot,) * 6,
        out_specs=(tok,) + (slot,) * 6,
        check_vma=False,
    )
```

time: 408 us -> 381 us (0.934)
  other arithmetic: 17.6 us -> 1.05 us
  Pallas kernels: 375 us -> 364 us
    pallas_call x2, Pallas kernels: 375 us -> 364 us  [the longest x1 358 us: shards(): pl.pallas_call(step_kernel, out_shape=[shape(N, 1024)] + [gu, buf] * 3 +...]
    convert_element_type x7 -> x2, other arithmetic: 10.5 us -> 0.02 us  [tables(): (x == k).astype(jnp.int32)]
    unnamed x23 -> x17, local copies, waits for them, and re-layouts: 8.16 us -> 12 us
where the time goes in v3:
time: 381 us; the launch traced here: 380 us
  Pallas kernels  364 us (96%)
  local copies, waits for them, and re-layouts  14.4 us (4%)
    pallas_call x1, Pallas kernels, shards(): pl.pallas_call(step_kernel, out_shape=[shape(N, 1024)] + [gu, buf] * 3 +...  358 us
    unnamed x17, local copies, waits for them, and re-layouts  12 us

profile of v3, /device:TPU:1, one launch (start us, length us, event | category | flops | bytes accessed | tf_op | source)
XLA Modules:
  0.0 380.3 jit_solution(2653312746492205777)
XLA Ops:
  0.6 0.8 reshape.369
  1.4 0.2 copy.29
  1.7 0.1 reshape.370
  1.8 0.1 eq.85
  1.9 0.8 select_reduce_fusion.1
  2.7 0.2 fusion
  3.0 1.2 stack.5.refs_0_
  4.2 1.4 copy.31.refs_3_
  5.6 1.4 copy.32.refs_4_
  7.0 358.2 %shard_map.189 = (bf16[128,1024]{1,0:T(8,128)(2,1)}, bf16[4,4,2,32,1024]{4,3,2,1,0:T(8,128)(2,1)}, bf16[4,4,2,16,1024]{4,3,2,1,0:T(8,128)(2,1)}, bf16[4,4,2,32,1...) custom-call(s32[9,128]{1,0:T(8,128)} %stack.5.refs_0_, ...), custom_call_target="tpu_custom_call" | custom-call | tf_op jit(solution)/shard_map/pallas_call | solution.py:534
  365.2 0.0 copy-start
  365.2 1.6 copy-done
  366.8 0.0 copy-start.1
  366.8 1.6 copy-done.1
  368.4 0.0 copy-start.2
  368.4 1.6 copy-done.2
  370.0 0.0 copy-start.3
  370.0 1.2 copy-done.3
  371.2 0.0 copy-start.4
  371.2 1.2 copy-done.4
  372.4 0.0 copy-start.5
  372.4 1.2 copy-done.5
  373.7 0.0 copy-start.6
  373.7 5.9 %shard_map.190 = (bf16[1,1024,1024]{2,1,0:T(8,128)(2,1)}, bf16[1,1024,1024]{2,1,0:T(8,128)(2,1)}, bf16[1,1024,1024]{2,1,0:T(8,128)(2,1)}, bf16[1,512,1024]{2,1,0...) custom-call(bf16[4,4,2,32,1024]{4,3,2,1,0:T(8,128)(2,1)S(1)} %copy-done, ...), custom_call_target="tpu_custom_call" | custom-call | tf_op jit(solution)/shard_map/pallas_call | solution.py:559
  379.6 0.0 copy-done.6
  379.6 0.7 copy.34
  (3 shorter events, 0.0 us)
Async XLA Ops:
  365.2 1.6 copy-start
  366.8 1.6 copy-start.1
  368.4 1.6 copy-start.2
  370.0 1.2 copy-start.3
  371.2 1.2 copy-start.4
  372.4 1.2 copy-start.5
  373.7 5.9 %copy-start.6 = (bf16[128,1024]{1,0:T(8,128)(2,1)S(1)}, bf16[128,1024]{1,0:T(8,128)(2,1)}, u32[]{:S(2)}) copy-start(bf16[128,1024]{1,0:T(8,128)(2,1)} %get-tuple-element.51) | copy-start | bytes 786436

commit v4 on v3

--- a/solution.py
+++ b/solution.py
@@ -15,6 +15,12 @@
 
 ORDER = (("x", "y", "z"), ("y", "z", "x"), ("z", "x", "y"))
 BUF = (4, 4, 2, 16, 1024)
+SLOTS = (2, 3, 2)
+
+X_WIDE = (384, 384, 256)
+C_WIDE = (384, 256, 384)
+Y_WIDE = (256, 384, 384)
+STEP = {"z": 32, "y": 8, "x": 2}
 
 
 def coordinates():
@@ -60,11 +66,10 @@
 
 
 class Exchanges:
-    def __init__(self, at, stages, sends, receives, bounces, bounce_sems):
-        self.at, self.stages = at, stages
+    def __init__(self, at, stages, near, sends, receives, bounces, bounce_sems):
+        self.at, self.stages, self.near = at, stages, near
         self.sends, self.receives = sends, receives
         self.bounces, self.bounce_sems = bounces, bounce_sems
-        self.slots = len(bounces) // 9
         self.held = {}
         self.drained = set()
         self.ids = {g: i for i, g in enumerate(stages)}
@@ -81,10 +86,17 @@
             mine = {axis: at[axis]}
             if phase == 0:
                 mine["c"] = at["c"]
+            if (g, phase) in self.near:
+                pltpu.make_async_copy(
+                    cut(src, src_rows, **mine),
+                    cut(dst, dst_rows, **mine),
+                    self.receives.at[i, s, phase],
+                ).start()
+                continue
             used = {v for k, v in self.held.items() if k[1:] == (s, phase)}
-            slot = min(set(range(self.slots)) - used)
+            slot = min(set(range(SLOTS[phase])) - used)
             self.held[g, s, phase] = slot
-            n = slot * 9 + s * 3 + phase
+            n = sum(SLOTS[:phase]) * 3 + slot * 3 + s
             load = pltpu.make_async_copy(
                 cut(src, src_rows, **mine), self.bounces[n], self.bounce_sems.at[n]
             )
@@ -120,7 +132,7 @@
         dst, rows = self.stages[g][s][phase + 1]
         whole = cut(dst, rows)
         pltpu.make_async_copy(whole, whole, self.receives.at[self.ids[g], s, phase]).wait()
-        del self.held[g, s, phase]
+        self.held.pop((g, s, phase), None)
 
     def finish(self, g):
         for s in range(3):
@@ -142,30 +154,85 @@
                 self.sent(g, phase)
 
 
-def to_pieces(back, rows48, store):
-    stacked = jnp.concatenate([rows48[:, q * 256 : q * 256 + 256] for q in range(4)], axis=0)
-    moved = jnp.dot(back, stacked, preferred_element_type=F32).astype(BF)
-    for s in range(3):
-        store(s, moved[s * 64 : s * 64 + 64].reshape(4, 16, 256))
-
-
-def from_pieces(there, refs, g, x):
-    parts = [
-        refs[s][g // 2, pl.ds(2 * (g % 2), 2), :, :, pl.ds(x * 256, 256)].reshape(64, 256)
-        for s in range(3)
-    ]
-    return jnp.dot(
-        there, jnp.concatenate(parts, axis=0), preferred_element_type=F32
-    ).astype(BF)
-
-
-def relayout(there, refs, out):
+def spans(wide):
+    return [(sum(wide[:s]), wide[s]) for s in range(3)]
+
+
+class TokenExchanges:
+    def __init__(self, at, sends, receives):
+        self.at, self.sends, self.receives = at, sends, receives
+
+    def _remote(self, src, dst, there, key, extra=0):
+        pltpu.make_async_remote_copy(
+            src,
+            dst,
+            self.sends.at[(*key, extra)],
+            self.receives.at[key],
+            device_id=device(self.at, **there),
+            device_id_type=MESH,
+        ).start()
+
+    def ring(self, g, phase, s, pairs, key=None):
+        axis = ORDER[s][0]
+        for d in (2, 1, 3):
+            there = (self.at[axis] + d) % 4
+            src, dst = pairs(there)
+            self._remote(src, dst, {axis: there}, key or (g, s, phase))
+
+    def second(self, g, phase, src, dst):
+        at = self.at
+        for d in (2, 1, 3, 0):
+            for dc in (0, 1):
+                for s in range(3):
+                    axis = ORDER[s][1]
+                    there = {axis: (at[axis] + d) % 4, "c": (at["c"] + dc) % 2}
+                    here = dst[s].at[at[axis], at["c"]]
+                    if d == 0 and dc == 0:
+                        pltpu.make_async_copy(
+                            src[s].at[at[axis], at["c"]], here, self.receives.at[g, s, phase]
+                        ).start()
+                    else:
+                        part = src[s].at[there[axis], there["c"]]
+                        self._remote(part, here, there, (g, s, phase), dc)
+
+    def third(self, g, phase, src, dst):
+        at = self.at
+        for d in (2, 1, 3, 0):
+            for s in range(3):
+                axis = ORDER[s][2]
+                to = (at[axis] + d) % 4
+                here = dst[s].at[:, :, at[axis]]
+                if d == 0:
+                    pltpu.make_async_copy(
+                        src[s].at[:, :, to], here, self.receives.at[g, s, phase]
+                    ).start()
+                else:
+                    self._remote(src[s].at[:, :, to], here, {axis: to}, (g, s, phase))
+
+    def arrived(self, g, phase, s, ref):
+        pltpu.make_async_copy(ref, ref, self.receives.at[g, s, phase]).wait()
+
+    def left(self, g, phase, s, ref, extra=0):
+        pltpu.make_async_copy(ref, ref, self.sends.at[g, s, phase, extra]).wait()
+
+
+def arrange(swap, land, wide, out):
     def body(g, carry):
-        for x in range(4):
-            moved = from_pieces(there, refs, g, x)
-            at = pl.multiple_of(x * 384 + g * 48, 16)
-            for q in range(4):
-                out[pl.ds(at, 48), q * 256 : q * 256 + 256] = moved[q * 48 : q * 48 + 48]
+        c = g % 2
+        for s, (start, n) in enumerate(spans(wide)):
+            cols = slice(start, start + n)
+            if s == 0:
+                out[pl.ds(pl.multiple_of(g * 192, 16), 192), cols] = land[s][g // 2, c].reshape(192, n)
+            elif s == 1:
+                rows = land[s][g // 2, c].reshape(192, n)
+                rows = jnp.dot(swap, rows, preferred_element_type=F32).astype(BF)
+                for y in range(4):
+                    r = pl.multiple_of(((y * 2 + c) * 4 + g // 2) * 48, 16)
+                    out[pl.ds(r, 48), cols] = rows[y * 48 : y * 48 + 48]
+            else:
+                rows = jnp.concatenate([land[s][x, c, g // 2] for x in range(4)], axis=0)
+                rows = jnp.dot(swap, rows, preferred_element_type=F32).astype(BF)
+                out[pl.ds(pl.multiple_of(g * 192, 16), 192), cols] = rows
         return carry
 
     lax.fori_loop(0, 8, body, 0)
@@ -176,60 +243,68 @@
     return sum(full[:, x * 256 : x * 256 + 256] * table[3 + x, j].astype(F32) for x in range(4))
 
 
-def routing(routes, gates, place, weighed):
+def routing(at, s, routes, gates, ranks, weights):
     lane = lax.broadcasted_iota(jnp.int32, (N, N), 1)
     line = lax.broadcasted_iota(jnp.int32, (N, N), 0)
-    slot = ((lane >> 3) & 3) * 32 + ((lane >> 1) & 3) * 8 + (lane >> 5) * 2 + (lane & 1)
+    first, second, third = ORDER[s]
+    slot = (line >> 5) * STEP[second] + ((line >> 4) & 1) + (line & 3) * STEP[third]
+    slot = slot + at[first] * STEP[first]
+    block = (line >> 2) & 3
     hit = jnp.zeros((N, N), F32)
     gate = jnp.zeros((N, N), F32)
-    for k in range(8):
-        named = routes[:, k : k + 1] == slot
-        hit = jnp.where(named, 1.0, hit)
-        gate = jnp.where(named, gates[:, k : k + 1], gate)
-    below = jnp.where(line > lane, 1.0, 0.0).astype(BF)
-    row = jnp.dot(below, hit.astype(BF), preferred_element_type=F32)
-    row = jnp.where(hit > 0.0, row, -1.0).T
-    gate = gate.T
-    high = gate.astype(BF)
-    rest = gate - high.astype(F32)
-    middle = rest.astype(BF)
-    low = (rest - middle.astype(F32)).astype(BF)
-    row = row.astype(BF)
-
-    def body(b, carry):
-        i = lax.broadcasted_iota(jnp.int32, (192, N), 0)
-        first = (lax.broadcasted_iota(jnp.int32, (192, N), 1) - b * 16) * CAP
-        spread = jnp.where((i >= first) & (i < first + CAP), 1.0, 0.0).astype(BF)
-        rank = i.astype(F32)
-        rank = rank - jnp.floor((rank + 0.5) * (1.0 / CAP)) * CAP
-
-        def copies(v):
-            return jnp.dot(spread, v, preferred_element_type=F32)
-
-        here = copies(row) == rank
-        r = pl.ds(pl.multiple_of(b * 192, 16), 192)
-        place[r] = jnp.where(here, 1.0, 0.0).astype(BF)
-        weighed[r] = jnp.where(here, copies(high) + copies(middle) + copies(low), 0.0)
-        return carry
-
-    lax.fori_loop(0, 8, body, 0)
+    for b in range(4):
+        wanted = jnp.where(block == b, slot, -1)
+        for k in range(8):
+            named = routes[b, k : k + 1, :] == wanted
+            hit = jnp.where(named, 1.0, hit)
+            gate = jnp.where(named, gates[b, k : k + 1, :], gate)
+    above = jnp.where(line < lane, 1.0, 0.0).astype(BF)
+    row = jnp.dot(hit.astype(BF), above, preferred_element_type=F32)
+    ranks[...] = jnp.where(hit > 0.0, row + 1.0, 0.0).astype(BF)
+    for part in range(3):
+        high = gate.astype(BF)
+        weights[part] = high
+        gate = gate - high.astype(F32)
+
+
+def placed(pick, ranks, g):
+    lines = pl.ds(pl.multiple_of(g * 16, 16), 16)
+    got = jnp.dot(pick, ranks[lines], preferred_element_type=F32)
+    i = lax.broadcasted_iota(jnp.int32, (192, N), 0).astype(F32)
+    rank = i - jnp.floor((i + 0.5) * (1.0 / CAP)) * CAP + 1.0
+    return [got[k * 192 : k * 192 + 192] == rank for k in range(4)]
+
+
+def weighed(pick, weights, here, g):
+    lines = pl.ds(pl.multiple_of(g * 16, 16), 16)
+    got = sum(
+        jnp.dot(pick, weights[part, lines], preferred_element_type=F32) for part in range(3)
+    )
+    return jnp.concatenate(
+        [jnp.where(here[k], got[k * 192 : k * 192 + 192], 0.0) for k in range(4)], axis=1
+    )
 
 
 def step_kernel(*refs):
-    table, there, back, routes, gates, tokens, cotangent = refs[:7]
+    table, swap, pick, routes, gates, tokens, cotangent = refs[:7]
     w_gu, w_dn, m_gu, m_dn, q_gu, q_dn = refs[7:13]
     layer_out, home_gu, home_dn = refs[13:16]
     new_m, new_q = refs[16:18], refs[18:20]
     m_far, q_far = refs[20:23], refs[23:26]
-    mids = refs[26:86]
-    scratch = refs[86:]
-    w_land, x_land, c_land, g_land, y_land = (scratch[i : i + 3] for i in range(0, 15, 3))
-    w_stage, x_send, c_send = (scratch[i : i + 3] for i in range(15, 24, 3))
-    gu, dn, g_gu, g_dn, xs, cs, hidden, d_pre, sums, place, weighed = scratch[24:35]
-    sends, receives, bounce_sems, copy_sem = scratch[35:39]
-    bounces = scratch[39:]
-    y_send, m_send, q_send = x_send, w_stage, c_send
-    m_old, q_old, ys = x_land, c_land, xs
+    mids = refs[26:68]
+    x_mid, c_mid, y_mid = refs[68:71], refs[71:74], refs[74:77]
+    scratch = refs[77:]
+    w_land, g_land, w_stage, old = (scratch[i : i + 3] for i in range(0, 12, 3))
+    x_send, c_send, x_land, c_land, y_land = (scratch[i : i + 3] for i in range(12, 27, 3))
+    x_all, c_all, y_parts = (scratch[i : i + 3] for i in range(27, 36, 3))
+    gu, dn, g_gu, g_dn, xs, cs, hidden, d_pre, sums = scratch[36:45]
+    all_routes, all_gates, ranks, weights, total, own = scratch[45:51]
+    sends, receives, bounce_sems, copy_sem, t_sends, t_receives = scratch[51:57]
+    bounces = scratch[57:]
+    m_send, q_send = w_stage, w_land
+    y_send = (x_send[2], x_send[0], x_send[1])
+    my_parts = (x_all[2], x_all[0], x_all[1])
+    y_kept = x_land[0]
 
     def raw(a, b):
         return [(a, 0), (a, 16), (b, None)]
@@ -239,13 +314,10 @@
 
     ends = {
         "w": (raw(w_gu, w_dn), plain(w_land)),
-        "x": (plain(x_send), plain(x_land)),
-        "c": (plain(c_send), plain(c_land)),
         "home": (plain(w_stage), raw(gu, dn)),
         "m": (raw(m_gu, m_dn), plain(m_far)),
         "q": (raw(q_gu, q_dn), plain(q_far)),
         "g": (raw(g_gu, g_dn), plain(g_land)),
-        "y": (plain(y_send), plain(y_land)),
         "new_m": (plain(m_send), raw(*new_m)),
         "new_q": (plain(q_send), raw(*new_q)),
     }
@@ -257,28 +329,71 @@
         ]
     at = coordinates()
     enter(at)
-    ex = Exchanges(at, stages, sends, receives, bounces, bounce_sems)
-
-    def pair(g):
-        return pl.ds(2 * (g % 2), 2)
-
-    def dispatch(rows, scaled, out):
+    near = {("w", 2), ("home", 0), ("home", 2), ("g", 0), ("g", 2), ("new_m", 0), ("new_q", 0)}
+    ex = Exchanges(at, stages, near, sends, receives, bounces, bounce_sems)
+    tx = TokenExchanges(at, t_sends, t_receives)
+
+    def gather(g, rows, everyone, wide):
+        for s, (start, n) in enumerate(spans(wide)):
+            here = everyone[s].at[at[ORDER[s][0]]]
+            mine = rows.at[:, pl.ds(start, n)]
+            tx.ring(g, 0, s, lambda there, mine=mine, here=here: (mine, here))
+
+    def keep_own(rows, everyone, wide):
+        for s, (start, n) in enumerate(spans(wide)):
+            everyone[s][at[ORDER[s][0]]] = rows[:, start : start + n]
+
+    def gather_tables():
+        for s in range(3):
+            me = at[ORDER[s][0]]
+            for k, (mine, everyone) in enumerate(((routes, all_routes), (gates, all_gates))):
+                here = everyone.at[s, me]
+                tx.ring(0, 0, s, lambda there, mine=mine, here=here: (mine, here), (3, s, k))
+                everyone[s, me] = mine[...]
+
+    def dispatch(s):
         def body(g, carry):
-            for x in range(4):
-                r = pl.ds(pl.multiple_of(x * 384 + g * 48, 16), 48)
-                got = jnp.dot(place[r], rows[...], preferred_element_type=F32)
-                if scaled:
-                    got = got * jnp.sum(weighed[r], axis=1, keepdims=True)
-
-                def store(s, value, x=x):
-                    out[s][g // 2, pair(g), :, :, x * 256 : x * 256 + 256] = value.reshape(
-                        2, 2, 16, 256
-                    )
-
-                to_pieces(back[...], got.astype(BF), store)
+            here = placed(pick[...], ranks.at[s], g)
+            place = jnp.concatenate(
+                [jnp.where(h, 1.0, 0.0).astype(BF) for h in here], axis=1
+            )
+            gate = jnp.sum(weighed(pick[...], weights.at[s], here, g), axis=1, keepdims=True)
+            for everyone, out, wide, factor in (
+                (x_all, x_send, X_WIDE, None),
+                (c_all, c_send, C_WIDE, gate),
+            ):
+                rows = everyone[s][...].reshape(512, wide[s])
+                got = jnp.dot(place, rows, preferred_element_type=F32)
+                if factor is not None:
+                    got = got * factor
+                out[s][g // 2, g % 2] = got.astype(BF).reshape(4, 48, wide[s])
             return carry
 
         lax.fori_loop(0, 8, body, 0)
+
+    def combine(s):
+        n = Y_WIDE[s]
+        total[...] = jnp.zeros_like(total)
+        over_rows = (((0,), (0,)), ((), ()))
+
+        def body(g, carry):
+            here = placed(pick[...], ranks.at[s], g)
+            weight = weighed(pick[...], weights.at[s], here, g)
+            high = weight.astype(BF)
+            low = (weight - high.astype(F32)).astype(BF)
+            rows = y_land[s][g // 2, g % 2].reshape(192, n)
+            got = lax.dot_general(high, rows, over_rows, preferred_element_type=F32)
+            got += lax.dot_general(low, rows, over_rows, preferred_element_type=F32)
+            total[:, 0:n] += got
+            return carry
+
+        lax.fori_loop(0, 8, body, 0)
+        start = spans(Y_WIDE)[s][0]
+        for k in range(4):
+            my_parts[s][k] = total[k * 128 : k * 128 + 128, 0:n].astype(BF)
+        me = at[ORDER[s][0]]
+        own[:, start : start + n] = total[pl.ds(pl.multiple_of(me * 128, 128), 128), 0:n]
+        tx.ring(2, 2, s, lambda there: (my_parts[s].at[there], y_parts[s].at[me]))
 
     def each_slot(do):
         def body(i, carry):
@@ -326,26 +441,47 @@
                 preferred_element_type=F32,
             )
         y = y.astype(BF)
-        cols = pl.ds(pl.multiple_of(b // 2 * 256, 256), 256)
-        for j in range(4):
-            g = b % 2 * 4 + j
-
-            def store(s, value):
-                y_send[s][g // 2, pair(j), :, :, cols] = value.reshape(2, 2, 16, 256)
-
-            to_pieces(back[...], y[j * 48 : j * 48 + 48], store)
+        (a0, an), (b0, bn), (c0, cn) = spans(Y_WIDE)
+        y_send[0][b // 2, b % 2] = y[:, a0 : a0 + an].reshape(4, 48, an)
+        y_kept[b // 2, b % 2] = y[:, b0 : b0 + bn].reshape(4, 48, bn)
+        rows = jnp.dot(swap[...], y[:, c0 : c0 + cn], preferred_element_type=F32).astype(BF)
+        for x in range(4):
+            y_send[2][x, b % 2, b // 2] = rows[x * 48 : x * 48 + 48]
         return carry
 
+    def turn(g, carry):
+        rows = jnp.concatenate([y_kept[y, g % 2, g // 2] for y in range(4)], axis=0)
+        rows = jnp.dot(swap[...], rows, preferred_element_type=F32).astype(BF)
+        y_send[1][g // 2, g % 2] = rows.reshape(4, 48, Y_WIDE[1])
+        return carry
+
+    def tokens_arrived(g, phase, refs):
+        for s in range(3):
+            tx.arrived(g, phase, s, refs[s])
+
+    def three(refs):
+        return [r.at[pl.ds(0, 3)] for r in refs]
+
+    gather_tables()
+    gather(0, tokens, x_all, X_WIDE)
+    gather(1, cotangent, c_all, C_WIDE)
     ex.start("w", 0)
     ex.start("m", 0)
-    routing(routes, gates, place, weighed)
-    dispatch(tokens, False, x_send)
+    keep_own(tokens, x_all, X_WIDE)
+    keep_own(cotangent, c_all, C_WIDE)
+    for s in range(3):
+        tx.arrived(3, 0, s, all_routes.at[s, pl.ds(0, 3)])
+        tx.arrived(3, 1, s, all_gates.at[s, pl.ds(0, 3)])
+        routing(at, s, all_routes.at[s], all_gates.at[s], ranks.at[s], weights.at[s])
+    tokens_arrived(0, 0, three(x_all))
+    tokens_arrived(1, 0, three(c_all))
+    dispatch(0)
     ex.start("w", 1)
-    ex.start("x", 0)
-    dispatch(cotangent, True, c_send)
+    dispatch(1)
+    dispatch(2)
+    tx.second(0, 1, x_send, x_mid)
     ex.start("w", 2)
-    ex.start("c", 0)
-    ex.start("x", 1)
+    tx.second(1, 1, c_send, c_mid)
     ex.start("m", 1)
     ex.finish("w")
 
@@ -354,25 +490,29 @@
 
     each_slot(select)
     ex.start("home", 0)
-    ex.start("c", 1)
-    ex.start("x", 2)
+    tokens_arrived(0, 1, x_mid)
+    tx.third(0, 2, x_mid, x_land)
     ex.start("home", 1)
-    ex.start("c", 2)
-    ex.start("q", 0)
+    tokens_arrived(1, 1, c_mid)
+    tx.third(1, 2, c_mid, c_land)
     ex.start("home", 2)
     ex.start("m", 2)
-    ex.finish("x")
-    relayout(there[...], x_land, xs)
-    ex.finish("c")
-    relayout(there[...], c_land, cs)
+    ex.start("q", 0)
+    tokens_arrived(0, 2, x_land)
+    arrange(swap[...], x_land, X_WIDE, xs)
+    tokens_arrived(1, 2, c_land)
+    arrange(swap[...], c_land, C_WIDE, cs)
+    ex.finish("home")
     ex.start("q", 1)
-    ex.finish("home")
     keep_gu = pltpu.make_async_copy(gu, home_gu, copy_sem.at[0])
     keep_dn = pltpu.make_async_copy(dn, home_dn, copy_sem.at[1])
     keep_gu.start()
     keep_dn.start()
-    ex.sent("x", 0)
+    for s in range(3):
+        tx.left(0, 1, s, x_mid[s].at[pl.ds(0, 3), 0], 0)
+        tx.left(0, 1, s, x_mid[s].at[:, 0], 1)
     lax.fori_loop(0, 8, forward, 0)
+    lax.fori_loop(0, 8, turn, 0)
     ex.start("q", 2)
     for k in range(4):
         got = lax.dot_general(
@@ -390,57 +530,79 @@
         )
         g_dn[k] = got.astype(BF).reshape(4, 2, 16, 1024)
     ex.start("g", 0)
-    ex.start("y", 0)
+    tx.third(2, 0, y_send, y_mid)
     ex.finish("m")
     ex.finish("q")
-    fetch = [
-        pltpu.make_async_copy(a, b, copy_sem.at[2 + i])
-        for i, (a, b) in enumerate(zip(m_far + q_far, m_old + q_old))
-    ]
-    for f in fetch:
-        f.start()
+
+    def fetch(far, first):
+        copies = [
+            pltpu.make_async_copy(a, b, copy_sem.at[first + i])
+            for i, (a, b) in enumerate(zip(far, old))
+        ]
+        for f in copies:
+            f.start()
+        return copies
+
+    coming = fetch(m_far, 2)
     ex.start("g", 1)
-    ex.start("y", 1)
+    tokens_arrived(2, 0, y_mid)
+    tx.second(2, 1, y_mid, y_land)
     ex.start("g", 2)
     for s in range(3):
         sums[s, N] = jnp.zeros((16, 256), F32)
+        tx.left(0, 0, s, x_all[s].at[pl.ds(0, 3)])
     ex.finish("g")
 
     def add(s, here, j):
         sums[s, j] = g_land[s][here].astype(F32) + sums[s, table[7, j]]
 
     each_slot(add)
-    ex.start("y", 2)
-    for f in fetch:
+    for f in coming:
         f.wait()
     ex.sent("home", 0)
-    ex.sent("c", 0)
 
     def update_first(s, here, j):
-        was = piece_of(m_old[s], table, j)
+        was = piece_of(old[s], table, j)
         m_send[s][here] = (0.9 * was + 0.1 * sums[s, table[8, j]]).astype(BF)
 
     def update_second(s, here, j):
-        was = piece_of(q_old[s], table, j)
+        was = piece_of(old[s], table, j)
         total = sums[s, table[8, j]]
         q_send[s][here] = (0.95 * was + 0.05 * total * total).astype(BF)
 
     each_slot(update_first)
     ex.start("new_m", 0)
+    for f in fetch(q_far, 5):
+        f.wait()
     each_slot(update_second)
     ex.start("new_q", 0)
+    tokens_arrived(2, 1, y_land)
+    combine(0)
     ex.start("new_m", 1)
-    ex.finish("y")
-    relayout(there[...], y_land, ys)
+    combine(1)
     ex.start("new_q", 1)
+    combine(2)
     ex.start("new_m", 2)
-    high = weighed[...].astype(BF)
-    low = (weighed[...] - high.astype(F32)).astype(BF)
-    over_rows = (((0,), (0,)), ((), ()))
-    mixed = lax.dot_general(high, ys[...], over_rows, preferred_element_type=F32)
-    mixed += lax.dot_general(low, ys[...], over_rows, preferred_element_type=F32)
-    layer_out[...] = mixed.astype(BF)
+    for s, (start, n) in enumerate(spans(Y_WIDE)):
+        tx.arrived(2, 2, s, y_parts[s].at[pl.ds(0, 3)])
+        me = at[ORDER[s][0]]
+        result = own[:, start : start + n]
+        for d in (1, 2, 3):
+            result += y_parts[s][(me + d) % 4].astype(F32)
+        layer_out[:, start : start + n] = result.astype(BF)
     ex.start("new_q", 2)
+    for s in range(3):
+        tx.left(1, 0, s, c_all[s].at[pl.ds(0, 3)])
+        tx.left(3, 0, s, all_routes.at[s, pl.ds(0, 3)])
+        tx.left(3, 1, s, all_gates.at[s, pl.ds(0, 3)])
+        tx.left(0, 2, s, x_mid[s].at[:, :, pl.ds(0, 3)])
+        tx.left(1, 1, s, c_mid[s].at[pl.ds(0, 3), 0], 0)
+        tx.left(1, 1, s, c_mid[s].at[:, 0], 1)
+        tx.left(1, 2, s, c_mid[s].at[:, :, pl.ds(0, 3)])
+        tx.left(2, 0, s, y_mid[s].at[:, :, pl.ds(0, 3)])
+        tx.left(2, 1, s, y_mid[s].at[pl.ds(0, 3), 0], 0)
+        tx.left(2, 1, s, y_mid[s].at[:, 0], 1)
+        tx.left(2, 2, s, y_parts[s].at[pl.ds(0, 3)])
     ex.finish("new_m")
     ex.finish("new_q")
     ex.drain()
@@ -465,26 +627,42 @@
     return jax.ShapeDtypeStruct(dims, dtype)
 
 
-def semaphores(groups, slots):
+def semaphores(groups):
     dma = pltpu.SemaphoreType.DMA
-    return [dma((groups, 3, 3)), dma((groups, 3, 3)), dma((slots * 9,)), dma((8,))]
-
-
-def bounce_buffers(slots):
+    return [
+        dma((groups, 3, 3)),
+        dma((groups, 3, 3)),
+        dma((sum(SLOTS) * 3,)),
+        dma((8,)),
+        dma((4, 3, 3, 2)),
+        dma((4, 3, 3)),
+    ]
+
+
+def bounce_buffers():
     return [
         pltpu.VMEM(bounce_shape(s, phase), BF)
-        for _ in range(slots)
+        for phase in range(3)
+        for _ in range(SLOTS[phase])
         for s in range(3)
-        for phase in range(3)
     ]
 
 
-def orders():
+def token_buffers(wide):
+    return [(4, 2, 4, 48, n) for n in wide]
+
+
+def constants():
     i = np.arange(192)
-    flat = i // 64 * 16 + i % 16
-    where_to = flat // 12 * 48 + (i % 64) // 16 * 12 + flat % 12
-    there = (i[:, None] == where_to[None, :]).astype(np.float32)
-    return jnp.asarray(there, BF), jnp.asarray(there.T, BF)
+    swap = (i // 12 % 4 * 48 + i // 48 * 12 + i % 12)[:, None] == i[None, :]
+    block = np.arange(4)[:, None, None]
+    line = np.arange(16)[None, None, :]
+    rows = i[None, :, None]
+    pick = (rows // 12 % 4 == block) & (line // 4 == block) & (line % 4 == rows // 48)
+    return (
+        jnp.asarray(swap.astype(np.float32), BF),
+        jnp.asarray(pick.reshape(768, 16).astype(np.float32), BF),
+    )
 
 
 def tables(old_experts, source):
@@ -515,7 +693,7 @@
     second_down,
 ):
     table = tables(old_experts, source)
-    there, back = orders()
+    swap, pick = constants()
     gu_shape, dn_shape = (4, 4, 2, 32, 1024), BUF
     arrays = (
         gate_up_weight.reshape(gu_shape),
@@ -530,24 +708,34 @@
     hbm = pl.BlockSpec(memory_space=pl.ANY)
     gu, buf = shape(*gu_shape), shape(*BUF)
     mega = 1 << 20
-    slots = 4
     outs = pl.pallas_call(
         step_kernel,
-        out_shape=[shape(N, 1024)] + [gu, buf] * 3 + [buf] * 66,
+        out_shape=[shape(N, 1024)]
+        + [gu, buf] * 3
+        + [buf] * 48
+        + [shape(*b) for wide in (X_WIDE, C_WIDE, Y_WIDE) for b in token_buffers(wide)],
         in_specs=[smem] + [vmem] * 6 + [hbm] * 6,
-        out_specs=[vmem] + [hbm] * 72,
-        scratch_shapes=[pltpu.VMEM(BUF, BF)] * 24
+        out_specs=[vmem] + [hbm] * 63,
+        scratch_shapes=[pltpu.VMEM(BUF, BF)] * 12
+        + [
+            pltpu.VMEM(b, BF)
+            for wide in (X_WIDE, C_WIDE, X_WIDE, C_WIDE, Y_WIDE)
+            for b in token_buffers(wide)
+        ]
+        + [pltpu.VMEM((4, 128, n), BF) for n in X_WIDE + C_WIDE + Y_WIDE]
         + [pltpu.VMEM(gu_shape, BF), pltpu.VMEM(BUF, BF)] * 2
         + [pltpu.VMEM((ROWS, 1024), BF)] * 2
         + [pltpu.VMEM((ROWS, 512), BF), pltpu.VMEM((ROWS, 1024), BF)]
         + [pltpu.VMEM((3, N + 1, 16, 256), F32)]
-        + [pltpu.VMEM((ROWS, N), BF), pltpu.VMEM((ROWS, N), F32)]
-        + semaphores(10, slots)
-        + bounce_buffers(slots),
+        + [pltpu.VMEM((3, 4, 8, N), jnp.int32), pltpu.VMEM((3, 4, 8, N), F32)]
+        + [pltpu.VMEM((3, N, N), BF), pltpu.VMEM((3, 3, N, N), BF)]
+        + [pltpu.VMEM((512, 384), F32), pltpu.VMEM((N, 1024), F32)]
+        + semaphores(7)
+        + bounce_buffers(),
         compiler_params=pltpu.CompilerParams(
             collective_id=0, has_side_effects=True, vmem_limit_bytes=63 * mega
         ),
-    )(table, there, back, routes, gate_weights, tokens, cotangent, *arrays)
+    )(table, swap, pick, routes.T, gate_weights.T, tokens, cotangent, *arrays)
     layer_out, home_gu, home_dn, m_gu, m_dn, q_gu, q_dn = outs[:7]
 
     def pieces(rows):
@@ -562,7 +750,7 @@
         out_shape=[shape(1, 1024, 1024)] * 3 + [shape(1, 512, 1024)] * 3,
         in_specs=[pieces(32)] * 3 + [pieces(16)] * 3,
         out_specs=[whole(128)] * 3 + [whole(64)] * 3,
-        compiler_params=pltpu.CompilerParams(vmem_limit_bytes=32 * mega),
+        compiler_params=pltpu.CompilerParams(vmem_limit_bytes=60 * mega),
     )(home_gu, m_gu, q_gu, home_dn, m_dn, q_dn)
     return layer_out, new[0], new[3], new[1], new[4], new[2], new[5]
 

time: 381 us -> 365 us (0.958)
  local copies, waits for them, and re-layouts: 14.4 us -> 3.18 us
  Pallas kernels: 364 us -> 360 us
    unnamed x17 -> x3, local copies, waits for them, and re-layouts: 12 us -> 0.71 us
    pallas_call x1, Pallas kernels: 358 us -> 349 us  [shards(): pl.pallas_call(step_kernel, out_shape=[shape(N, 1024)] + [gu, buf] * 3 +...]
    pallas_call x1, Pallas kernels: 5.9 us -> 10.3 us  [shards(): pl.pallas_call(weights_kernel, grid=(8,), out_shape=[shape(1, 1024, 1024)...]
where the time goes in v4:
time: 365 us
  Pallas kernels  360 us (99%)
    pallas_call x1, Pallas kernels, shards(): pl.pallas_call(step_kernel, out_shape=[shape(N, 1024)] + [gu, buf] * 3 +...  349 us
    pallas_call x1, Pallas kernels, shards(): pl.pallas_call(weights_kernel, grid=(8,), out_shape=[shape(1, 1024, 1024)...  10.3 us

profile of v4, /device:TPU:1, one launch (start us, length us, event | category | flops | bytes accessed | tf_op | source)
XLA Modules:
  0.0 364.5 jit_solution(14608964097044775526)
XLA Ops:
  0.6 0.8 reshape.369
  1.4 0.2 copy.25
  1.7 0.1 reshape.370
  1.8 0.1 eq.85
  1.9 0.8 select_reduce_fusion.1
  2.7 0.2 fusion
  3.0 1.2 stack.5.refs_0_
  4.2 349.3 %shard_map.189 = (bf16[128,1024]{1,0:T(8,128)(2,1)}, bf16[4,4,2,32,1024]{4,3,2,1,0:T(8,128)(2,1)}, bf16[4,4,2,16,1024]{4,3,2,1,0:T(8,128)(2,1)}, bf16[4,4,2,32,1...) custom-call(s32[9,128]{1,0:T(8,128)} %stack.5.refs_0_, ...), custom_call_target="tpu_custom_call" | custom-call | tf_op jit(solution)/shard_map/pallas_call | solution.py:711
  353.5 0.0 copy-start
  353.5 10.3 %shard_map.190 = (bf16[1,1024,1024]{2,1,0:T(8,128)(2,1)}, bf16[1,1024,1024]{2,1,0:T(8,128)(2,1)}, bf16[1,1024,1024]{2,1,0:T(8,128)(2,1)}, bf16[1,512,1024]{2,1,0...) custom-call(bf16[4,4,2,32,1024]{4,3,2,1,0:T(8,128)(2,1)} %get-tuple-element.21.refs_0_, ...), custom_call_target="tpu_custom_call" | custom-call | tf_op jit(solution)/shard_map/pallas_call | solution.py:747
  363.8 0.0 copy-done
  363.8 0.7 copy.28
  (3 shorter events, 0.0 us)
Async XLA Ops:
  353.5 10.4 %copy-start = (bf16[128,1024]{1,0:T(8,128)(2,1)S(1)}, bf16[128,1024]{1,0:T(8,128)(2,1)}, u32[]{:S(2)}) copy-start(bf16[128,1024]{1,0:T(8,128)(2,1)} %get-tuple-element.51) | copy-start | bytes 786436

commit v5 on v4

--- a/solution.py
+++ b/solution.py
@@ -462,10 +462,10 @@
     def three(refs):
         return [r.at[pl.ds(0, 3)] for r in refs]
 
+    ex.start("w", 0)
     gather_tables()
     gather(0, tokens, x_all, X_WIDE)
     gather(1, cotangent, c_all, C_WIDE)
-    ex.start("w", 0)
     ex.start("m", 0)
     keep_own(tokens, x_all, X_WIDE)
     keep_own(cotangent, c_all, C_WIDE)
@@ -482,7 +482,6 @@
     tx.second(0, 1, x_send, x_mid)
     ex.start("w", 2)
     tx.second(1, 1, c_send, c_mid)
-    ex.start("m", 1)
     ex.finish("w")
 
     def select(s, here, j):
@@ -496,14 +495,13 @@
     tokens_arrived(1, 1, c_mid)
     tx.third(1, 2, c_mid, c_land)
     ex.start("home", 2)
-    ex.start("m", 2)
+    ex.start("m", 1)
     ex.start("q", 0)
     tokens_arrived(0, 2, x_land)
     arrange(swap[...], x_land, X_WIDE, xs)
     tokens_arrived(1, 2, c_land)
     arrange(swap[...], c_land, C_WIDE, cs)
     ex.finish("home")
-    ex.start("q", 1)
     keep_gu = pltpu.make_async_copy(gu, home_gu, copy_sem.at[0])
     keep_dn = pltpu.make_async_copy(dn, home_dn, copy_sem.at[1])
     keep_gu.start()
@@ -512,8 +510,9 @@
         tx.left(0, 1, s, x_mid[s].at[pl.ds(0, 3), 0], 0)
         tx.left(0, 1, s, x_mid[s].at[:, 0], 1)
     lax.fori_loop(0, 8, forward, 0)
+    ex.start("m", 2)
+    ex.start("q", 1)
     lax.fori_loop(0, 8, turn, 0)
-    ex.start("q", 2)
     for k in range(4):
         got = lax.dot_general(
             xs[:, k * 256 : k * 256 + 256],
@@ -531,8 +530,6 @@
         g_dn[k] = got.astype(BF).reshape(4, 2, 16, 1024)
     ex.start("g", 0)
     tx.third(2, 0, y_send, y_mid)
-    ex.finish("m")
-    ex.finish("q")
 
     def fetch(far, first):
         copies = [
@@ -543,11 +540,13 @@
             f.start()
         return copies
 
+    ex.start("g", 1)
+    ex.start("q", 2)
+    ex.finish("m")
     coming = fetch(m_far, 2)
-    ex.start("g", 1)
+    ex.start("g", 2)
     tokens_arrived(2, 0, y_mid)
     tx.second(2, 1, y_mid, y_land)
-    ex.start("g", 2)
     for s in range(3):
         sums[s, N] = jnp.zeros((16, 256), F32)
         tx.left(0, 0, s, x_all[s].at[pl.ds(0, 3)])
@@ -572,6 +571,7 @@
 
     each_slot(update_first)
     ex.start("new_m", 0)
+    ex.finish("q")
     for f in fetch(q_far, 5):
         f.wait()
     each_slot(update_second)

time: 365 us -> 346 us (0.948)
  Pallas kernels: 360 us -> 340 us
    pallas_call x1, Pallas kernels: 349 us -> 330 us  [shards(): pl.pallas_call(step_kernel, out_shape=[shape(N, 1024)] + [gu, buf] * 3 +...]
where the time goes in v5:
time: 346 us; the launch traced here: 345 us
  Pallas kernels  340 us (98%)
    pallas_call x1, Pallas kernels, shards(): pl.pallas_call(step_kernel, out_shape=[shape(N, 1024)] + [gu, buf] * 3 +...  330 us
    pallas_call x1, Pallas kernels, shards(): pl.pallas_call(weights_kernel, grid=(8,), out_shape=[shape(1, 1024, 1024)...  10.3 us

profile of v5, /device:TPU:1, one launch (start us, length us, event | category | flops | bytes accessed | tf_op | source)
XLA Modules:
  0.0 345.0 jit_solution(14173519131220124091)
XLA Ops:
  0.6 0.8 reshape.369
  1.4 0.2 copy.25
  1.7 0.1 reshape.370
  1.8 0.1 eq.85
  1.9 0.8 select_reduce_fusion.1
  2.7 0.2 fusion
  3.0 1.2 stack.5.refs_0_
  4.2 329.7 %shard_map.189 = (bf16[128,1024]{1,0:T(8,128)(2,1)}, bf16[4,4,2,32,1024]{4,3,2,1,0:T(8,128)(2,1)}, bf16[4,4,2,16,1024]{4,3,2,1,0:T(8,128)(2,1)}, bf16[4,4,2,32,1...) custom-call(s32[9,128]{1,0:T(8,128)} %stack.5.refs_0_, ...), custom_call_target="tpu_custom_call" | custom-call | tf_op jit(solution)/shard_map/pallas_call | solution.py:711
  333.9 0.0 copy-start
  334.0 10.3 %shard_map.190 = (bf16[1,1024,1024]{2,1,0:T(8,128)(2,1)}, bf16[1,1024,1024]{2,1,0:T(8,128)(2,1)}, bf16[1,1024,1024]{2,1,0:T(8,128)(2,1)}, bf16[1,512,1024]{2,1,0...) custom-call(bf16[4,4,2,32,1024]{4,3,2,1,0:T(8,128)(2,1)} %get-tuple-element.21.refs_0_, ...), custom_call_target="tpu_custom_call" | custom-call | tf_op jit(solution)/shard_map/pallas_call | solution.py:747
  344.3 0.0 copy-done
  344.3 0.7 copy.28
  (3 shorter events, 0.0 us)
Async XLA Ops:
  333.9 10.4 %copy-start = (bf16[128,1024]{1,0:T(8,128)(2,1)S(1)}, bf16[128,1024]{1,0:T(8,128)(2,1)}, u32[]{:S(2)}) copy-start(bf16[128,1024]{1,0:T(8,128)(2,1)} %get-tuple-element.51) | copy-start | bytes 786436

commit v6 on v5

--- a/solution.py
+++ b/solution.py
@@ -509,8 +509,9 @@
     for s in range(3):
         tx.left(0, 1, s, x_mid[s].at[pl.ds(0, 3), 0], 0)
         tx.left(0, 1, s, x_mid[s].at[:, 0], 1)
-    lax.fori_loop(0, 8, forward, 0)
+    lax.fori_loop(0, 4, forward, 0)
     ex.start("m", 2)
+    lax.fori_loop(4, 8, forward, 0)
     ex.start("q", 1)
     lax.fori_loop(0, 8, turn, 0)
     for k in range(4):

time: 346 us -> 346 us (level)
  no operation moved by 1% of the time
where the time goes in v6:
time: 346 us; the launch traced here: 345 us
  Pallas kernels  340 us (98%)
    pallas_call x1, Pallas kernels, shards(): pl.pallas_call(step_kernel, out_shape=[shape(N, 1024)] + [gu, buf] * 3 +...  330 us
    pallas_call x1, Pallas kernels, shards(): pl.pallas_call(weights_kernel, grid=(8,), out_shape=[shape(1, 1024, 1024)...  10.3 us

profile of v6, /device:TPU:1, one launch (start us, length us, event | category | flops | bytes accessed | tf_op | source)
XLA Modules:
  0.0 345.0 jit_solution(2831371219539863273)
XLA Ops:
  0.6 0.8 reshape.369
  1.4 0.2 copy.25
  1.7 0.1 reshape.370
  1.8 0.1 eq.85
  1.9 0.8 select_reduce_fusion.1
  2.7 0.2 fusion
  3.0 1.2 stack.5.refs_0_
  4.2 329.7 %shard_map.189 = (bf16[128,1024]{1,0:T(8,128)(2,1)}, bf16[4,4,2,32,1024]{4,3,2,1,0:T(8,128)(2,1)}, bf16[4,4,2,16,1024]{4,3,2,1,0:T(8,128)(2,1)}, bf16[4,4,2,32,1...) custom-call(s32[9,128]{1,0:T(8,128)} %stack.5.refs_0_, ...), custom_call_target="tpu_custom_call" | custom-call | tf_op jit(solution)/shard_map/pallas_call | solution.py:712
  333.9 0.0 copy-start
  334.0 10.3 %shard_map.190 = (bf16[1,1024,1024]{2,1,0:T(8,128)(2,1)}, bf16[1,1024,1024]{2,1,0:T(8,128)(2,1)}, bf16[1,1024,1024]{2,1,0:T(8,128)(2,1)}, bf16[1,512,1024]{2,1,0...) custom-call(bf16[4,4,2,32,1024]{4,3,2,1,0:T(8,128)(2,1)} %get-tuple-element.21.refs_0_, ...), custom_call_target="tpu_custom_call" | custom-call | tf_op jit(solution)/shard_map/pallas_call | solution.py:748
  344.3 0.0 copy-done
  344.3 0.7 copy.28
  (3 shorter events, 0.0 us)
Async XLA Ops:
  333.9 10.4 %copy-start = (bf16[128,1024]{1,0:T(8,128)(2,1)S(1)}, bf16[128,1024]{1,0:T(8,128)(2,1)}, u32[]{:S(2)}) copy-start(bf16[128,1024]{1,0:T(8,128)(2,1)} %get-tuple-element.51) | copy-start | bytes 786436
